TPU v7x, 256 devices: a whole 4x4x8 slice. The times are simulated.
256 devices in a mesh: worker: 8 (over z_lo, x), shard: 32 (over z_hi, y, core).
Axes of the slice: x: 4, y: 4, z: 8 (z_hi: 4, z_lo: 2; z = z_hi * 2 + z_lo), core: 2. Of those that a mesh axis runs over, the one named last changes fastest.
Arguments:
- acts: bfloat16 [131072, 8192], P(('worker', 'shard')), may hold values from -6 to 6
- out_grads: bfloat16 [131072, 1024], P(('worker', 'shard')), may hold values from -24 to 24
- local_weight: bfloat16 [8, 1024, 8192], P('worker', 'shard'), may hold values from -6.1 to 6.1
- adam_mean: float32 [8, 1024, 8192], P('worker', 'shard'), may hold values from -0.6 to 0.6
- adam_var: float32 [8, 1024, 8192], P('worker', 'shard'), may hold values from 0.05 to 2
- global_weight: float32 [1024, 8192], P('shard', 'worker'), may hold values from -6 to 6
- outer_momentum: float32 [1024, 8192], P('shard', 'worker'), may hold values from -0.12 to 0.12
- step_count: int32 [1], replicated, may hold values from 1 to 8
Outputs:
- synced_weight: bfloat16 [1024, 8192], P('shard')
- new_global: float32 [1024, 8192], P('shard', 'worker')
- new_momentum: float32 [1024, 8192], P('shard', 'worker')
All inputs are finite; a program needn't handle non-finite values.
Results may differ from a plain program's by a relative error of at most 0.012.
Values may be sent and summed in bfloat16 or wider, within the bound.
No kernel may reach another device: no remote copies, remote signals or barrier semaphores. Data moves between devices by JAX's collectives and lax.ppermute only.
A program may use at most 128 MiB of HBM per device.

v0:
```python
import math

import jax
import jax.numpy as jnp
from jax import lax
from jax.sharding import PartitionSpec as P


def inner_step(weight, mean, var, grad, count):
    moment = 0.9 * mean + 0.1 * grad
    second = 0.95 * var + 0.05 * grad * grad
    first_fix = 1.0 - jnp.power(0.9, count)
    second_fix = 1.0 - jnp.power(0.95, count)
    ratio = moment / first_fix / (jnp.sqrt(second / second_fix) + 1e-08)
    return weight - 0.1 * (ratio + 0.1 * weight)


def local(
    acts, out_grads, local_weight, adam_mean, adam_var, global_weight, outer_momentum, step_count
):
    shards = lax.axis_size("shard")
    workers = lax.axis_size("worker")
    units = local_weight.shape[1]
    tokens = acts.shape[0]
    factor = 1.0 / math.sqrt(tokens * shards)
    count = step_count[0].astype(jnp.float32)
    blocks = 1
    share = units // blocks
    arranged = out_grads.reshape(tokens, shards, blocks, share)
    picked = arranged[:, :, 0, :].reshape(tokens, shards * share)

    def gradient_term(start, rows, picked=picked):
        return (
            lax.dot_general(
                picked, acts, (((0,), (0,)), ((), ())), preferred_element_type=jnp.float32
            )
            * factor
        )

    grad = lax.psum_scatter(
        gradient_term(jnp.int32(0), lax.axis_size("shard") * share).astype(jnp.bfloat16),
        "shard",
        scatter_dimension=0,
        tiled=True,
    ).astype(jnp.float32)
    weight = local_weight[0, 0:share].astype(jnp.float32)
    stepped = inner_step(weight, adam_mean[0, 0:share], adam_var[0, 0:share], grad, count)
    summed = lax.psum_scatter(stepped, "worker", scatter_dimension=1, tiled=True)
    delta = global_weight - summed / workers
    momentum = 0.9 * outer_momentum + delta
    updated = global_weight - 0.7 * (delta + 0.9 * momentum)
    synced = lax.all_gather(updated.astype(jnp.bfloat16), "worker", axis=1, tiled=True)
    return (synced, updated, momentum)


def solution(mesh):
    placed = (
        P(("worker", "shard"), None),
        P(("worker", "shard"), None),
        P("worker", "shard", None),
        P("worker", "shard", None),
        P("worker", "shard", None),
        P("shard", "worker"),
        P("shard", "worker"),
        P(),
    )
    return jax.shard_map(
        local,
        mesh=mesh,
        in_specs=placed,
        out_specs=(P("shard", None), P("shard", "worker"), P("shard", "worker")),
        check_vma=False,
    )
```

profile of v0, /device:TPU:64, one launch (start us, length us, event | category | flops | bytes accessed | tf_op | source)
XLA Modules:
  0.0 275.8 jit_solution(5612209698980541747)
XLA Ops:
  7.2 0.0 copy-start
  7.2 0.0 copy-start.1
  7.2 0.0 copy-start.2
  7.2 0.0 reduce-scatter.3.cloned.1.call-start
  7.2 1.1 copy-done
  8.4 15.8 %multiply_convert_fusion = bf16[1024,8192]{1,0:T(8,128)(2,1)} fusion(bf16[512,1024]{1,0:T(8,128)(2,1)S(1)} %copy-done, bf16[512,8192]{1,0:T(8,128)(2,1)} %param.8), kind=kOutput, calls=%fused_computation | convolution fusion | flops 8606711808 | bytes 26214400 | tf_op jit(solution)/shard_map/dot_general | solution.py:34
  24.2 0.0 copy-start.3
  24.2 0.0 copy-start.4
  24.2 0.0 reduce-scatter.3.cloned.1.call-update
  24.2 0.0 reduce-scatter.5.cloned.1.call-start
  25.0 167.7 %reduce-scatter.3.cloned.1.call-done = bf16[32,8192]{1,0:T(8,128)(2,1)} async-done(((bf16[1024,8192]{1,0:T(8,128)(2,1)}), bf16[32,8192]{1,0:T(8,128)(2,1)}) %reduce-scatter.3.cloned.1.call-update) | async-done | bytes 524304 | tf_op jit(solution)/shard_map/reduce_scatter | solution.py:40
  192.8 0.0 copy-done.1
  192.8 0.0 copy-done.2
  192.8 3.0 %convert_subtract_fusion = f32[32,8192]{1,0:T(8,128)} fusion(bf16[32,8192]{1,0:T(8,128)(2,1)} %reduce-scatter.3.cloned.1.call-done, f32[1,32,8192]{2,1,0:T(8,128)S(1)} %copy-done.1, f32[1,32,8192]{2,1,0:T(8,128)S(1)} %copy-done.2, bf16[1,32,8192]{2,1,0:T(8,128)(2,1)} %param.10, f32[]{:T(128)} %bitcast.4, f32[]{:T(128)} %bitcast.2), kind=kLoop, calls=%fused_computation.2 | loop fusion | flops 4456448 | bytes 4194312 | tf_op jit(solution)/shard_map/sub | solution.py:15
  195.8 0.0 reduce-scatter.5.cloned.1.call-update
  195.8 41.6 %reduce-scatter.5.cloned.1.call-done = f32[32,1024]{1,0:T(8,128)} async-done(((f32[32,8192]{1,0:T(8,128)}), f32[32,1024]{1,0:T(8,128)}) %reduce-scatter.5.cloned.1.call-update) | async-done | bytes 131088 | tf_op jit(solution)/shard_map/reduce_scatter | solution.py:48
  237.4 0.0 copy-done.3
  237.4 0.0 copy-done.4
  237.4 1.6 fusion.9
  239.1 29.1 %all_gather.3 = bf16[32,8192]{1,0:T(8,128)(2,1)S(1)} all-gather(bf16[32,1024]{1,0:T(8,128)(2,1)S(1)} %get-tuple-element.3), channel_id=1, replica_groups=mesh['worker'=8,'shard'=32] {'worker'}, dimensions={1}, use_global_device_ids=true | all-gather | bytes 589824 | tf_op jit(solution)/shard_map/all_gather | solution.py:52
  268.1 0.8 copy.13
Async XLA Ops:
  7.2 1.2 copy-start
  7.2 185.6 %copy-start.1 = (f32[1,32,8192]{2,1,0:T(8,128)S(1)}, f32[1,32,8192]{2,1,0:T(8,128)}, u32[]{:S(2)}) copy-start(f32[1,32,8192]{2,1,0:T(8,128)} %param.12) | copy-start | bytes 3145732
  7.2 185.6 %copy-start.2 = (f32[1,32,8192]{2,1,0:T(8,128)S(1)}, f32[1,32,8192]{2,1,0:T(8,128)}, u32[]{:S(2)}) copy-start(f32[1,32,8192]{2,1,0:T(8,128)} %param.11) | copy-start | bytes 3145732
  7.2 185.6 %reduce-scatter.3.cloned.1.call-start = ((), (), s32[]{:S(2)}) async-start(), calls=%async_computation.2 | async-start | bytes 17301504 | tf_op jit(solution)/shard_map/reduce_scatter | solution.py:40
  24.2 213.2 %copy-start.3 = (f32[32,1024]{1,0:T(8,128)S(1)}, f32[32,1024]{1,0:T(8,128)}, u32[]{:S(2)}) copy-start(f32[32,1024]{1,0:T(8,128)} %param.13) | copy-start | bytes 393220
  24.2 213.2 %copy-start.4 = (f32[32,1024]{1,0:T(8,128)S(1)}, f32[32,1024]{1,0:T(8,128)}, u32[]{:S(2)}) copy-start(f32[32,1024]{1,0:T(8,128)} %param.14) | copy-start | bytes 393220
  24.2 213.2 %reduce-scatter.5.cloned.1.call-start = ((), (), s32[]{:S(2)}) async-start(), calls=%async_computation.3 | async-start | bytes 1179648 | tf_op jit(solution)/shard_map/reduce_scatter | solution.py:48
Sparse Core Ops, SparseCore 0:
  24.3 168.3 reduce-scatter.2
  195.9 41.4 reduce-scatter.4
where the time goes:
time: 277 us; the launch traced here: 276 us
  waiting for transfers between devices  209 us (75%)
  blocking collectives  29.1 us (11%)
  matrix products  15.8 us (6%)
  between operations  14.8 us (5%)
  other arithmetic  4.67 us (2%)
    reduce_scatter x1, waiting for transfers between devices, local(): lax.psum_scatter(gradient_term(jnp.int32(0), lax.axis_size('shard') * sha...  168 us
    reduce_scatter x1, waiting for transfers between devices, local(): lax.psum_scatter(stepped, 'worker', scatter_dimension=1, tiled=True)  41.6 us
    all_gather x1, blocking collectives, local(): lax.all_gather(updated.astype(jnp.bfloat16), 'worker', axis=1, tiled=True)  29.1 us
    dot_general x1, matrix products, gradient_term(): lax.dot_general(picked, acts, (((0,), (0,)), ((), ())), preferred_element...  15.8 us
  transfers between devices with their start and end apart: 2, of which 2 were waited for; matrix products, arithmetic and copies ran while one was open for 0% of the time, Pallas kernels for 0%

commit v1 on v0

v1 whole, which is shorter than its diff:
```python
import functools
import math

import jax
import jax.numpy as jnp
from jax import lax
from jax.experimental import pallas as pl
from jax.experimental.pallas import tpu as pltpu
from jax.sharding import PartitionSpec as P

WIDTHS = {"a": 2304, "b": 2304, "c": 1024, "d": 1024, "e": 1536}

NZ, NY, NC = 4, 4, 2
SHARDS = NZ * NY * NC
BACK = (1, 2, 3, 0)
VMEM = pl.BlockSpec(memory_space=pltpu.VMEM)
LIMIT = 16 << 20
bf16, f32 = jnp.bfloat16, jnp.float32


def shard_of(z, y, c):
    return (z % NZ * NY + y % NY) * NC + c % NC


def sense(c):
    return 1 if c == 0 else -1


def move(array, axis, steps=1):
    pairs = []
    for z in range(NZ):
        for y in range(NY):
            for c in range(NC):
                by = steps * sense(c)
                to = {
                    "z": shard_of(z + by, y, c), "y": shard_of(z, y + by, c), "core": shard_of(z, y, c + 1)
                }[axis]
                pairs.append((shard_of(z, y, c), to))
    return lax.ppermute(array, "shard", pairs)


class Line:
    def __init__(self):
        self.last = None

    def call(self, kernel, name, outs, *operands, scalars=(), flops=0):
        size = sum(o.size * o.dtype.itemsize for o in operands) + sum(
            math.prod(s) * jnp.dtype(t).itemsize for s, t in outs
        )
        before = () if self.last is None else (self.last,)
        skip = len(before)
        results = pl.pallas_call(
            lambda *refs: kernel(*refs[skip:]),
            out_shape=[jax.ShapeDtypeStruct(s, t) for s, t in outs],
            in_specs=[pl.BlockSpec(memory_space=pl.ANY)] * skip
            + [pl.BlockSpec(memory_space=pltpu.SMEM)] * len(scalars)
            + [VMEM] * len(operands),
            out_specs=[VMEM] * len(outs),
            compiler_params=pltpu.CompilerParams(vmem_limit_bytes=LIMIT),
            cost_estimate=pl.CostEstimate(flops=0, bytes_accessed=0, transcendentals=0),
            name=name,
        )(*before, *scalars, *operands)
        self.last = results[0]
        return results


def pick_kernel(factor, feature_ref, grads_ref, out_ref):
    shape = (feature_ref.shape[0], grads_ref.shape[1])
    match = feature_ref[...] == lax.broadcasted_iota(jnp.int32, shape, 1)
    pick = jnp.where(match, factor, 0.0).astype(bf16)
    out_ref[...] = lax.dot_general(
        pick, grads_ref[...], (((1,), (1,)), ((), ())), preferred_element_type=f32
    ).astype(bf16)


def product_kernel(split, gm_ref, gs_ref, mine_ref, sib_ref, *outs):
    cols = mine_ref.shape[1]
    tile = 256
    for start in range(0, cols, tile):
        part = pl.ds(start, tile)
        mine, sib = mine_ref[:, part], sib_ref[:, part]
        total = jnp.dot(gm_ref[...], mine, preferred_element_type=f32)
        total += jnp.dot(gs_ref[...], sib, preferred_element_type=f32)
        for out, rows in zip(outs, split):
            out[:, part] = jnp.concatenate([total[r] for r in rows], axis=0).astype(out.dtype)


def relay_kernel(keep_ref, came_ref, out_ref):
    out_ref[...] = (keep_ref[...] + came_ref[...].astype(f32)).astype(bf16)


def settle_kernel(n, *refs):
    ins, outs = refs[:2 * n], refs[2 * n:]
    start = 0
    for own, came in zip(ins[::2], ins[1::2]):
        part = slice(start, start + own.shape[1])
        start += own.shape[1]
        rows = own.shape[0] // len(outs)
        for i, out in enumerate(outs):
            at = slice(i * rows, (i + 1) * rows)
            out[:, part] = (own[at] + came[at].astype(f32)).astype(out.dtype)


def adam_kernel(start, fix_ref, weight_ref, mean_ref, var_ref, own_ref, *refs):
    came, out_ref = refs[:-1], refs[-1]
    at = pl.ds(start, own_ref.shape[1])
    grad = own_ref[...]
    for ref in came:
        grad += ref[...].astype(f32)
    weight = weight_ref[:, at].astype(f32)
    moment = 0.9 * mean_ref[:, at] + 0.1 * grad
    second = 0.95 * var_ref[:, at] + 0.05 * grad * grad
    ratio = moment / fix_ref[0] / (jnp.sqrt(second / fix_ref[1]) + 1e-08)
    out_ref[...] = weight - 0.1 * (ratio + 0.1 * weight)


def after(array, *others):
    return lax.optimization_barrier((array,) + others)[0]


def local(acts, out_grads, local_weight, adam_mean, adam_var, global_weight, outer_momentum, step_count):
    workers = lax.axis_size("worker")
    tokens, width = acts.shape
    features = out_grads.shape[1]
    share = features // SHARDS
    half = features // NC
    rows = half // NY
    factor = 1.0 / math.sqrt(tokens * SHARDS)
    count = step_count[0].astype(f32)
    index = lax.axis_index("shard")
    core, y, z = index % NC, (index // NC) % NY, index // (NC * NY)

    offsets, total = {}, 0
    for k, cols in WIDTHS.items():
        offsets[k] = total
        total += cols

    back = jnp.array(BACK, jnp.int32) * jnp.where(core == 0, 1, -1)
    owner = ((z - back[None, :]) % NZ * NY + (y - back[:, None]) % NY) * NC + core
    feature = (owner.reshape(-1, 1) * share + jnp.arange(share, dtype=jnp.int32)[None, :]).reshape(half, 1)
    fix = jnp.stack([1.0 - jnp.power(0.9, count), 1.0 - jnp.power(0.95, count)])
    line = Line()

    def picked(grads):
        return line.call(
            functools.partial(pick_kernel, factor), "pick", [((half, tokens), bf16)], feature, grads
        )[0]

    mine, sib, blocks, flying = ({} for _ in range(4))
    weights = (local_weight[0], adam_mean[0], adam_var[0])
    by_y = [[slice(i * rows, (i + 1) * rows)] for i in range(NY)]
    by_z = [[slice((j * NZ + i) * share, (j * NZ + i + 1) * share) for j in range(NY)] for i in range(NZ)]

    def fetch(k, *others):
        mine[k] = lax.slice_in_dim(after(acts, *others), offsets[k], offsets[k] + WIDTHS[k], axis=1)
        sib[k] = move(mine[k], "core")

    def send(k, message, axis):
        flying[k] = move(message, axis)

    def produce(k, axis):
        out = ((rows, WIDTHS[k]), bf16), *[((rows, WIDTHS[k]), f32)] * 3
        message, *blocks[k] = line.call(
            functools.partial(product_kernel, by_y if axis == "y" else by_z), "product", out,
            gm, gs, mine[k], sib[k],
        )
        send(k, message, axis)

    def relay(k, axis):
        keep = blocks[k].pop(0)
        send(k, line.call(relay_kernel, "relay", [(keep.shape, bf16)], keep, flying[k])[0], axis)

    def settle(ks, axis, direct=False):
        cols = sum(WIDTHS[k] for k in ks)
        out = [((share, cols), bf16)] + [((share, cols), bf16 if direct else f32)] * 2 + [((share, cols), f32)]
        message, *blocks[ks] = line.call(
            functools.partial(settle_kernel, len(ks)), "settle", out,
            *[a for k in ks for a in (blocks[k][0], flying[k])],
        )
        if direct:
            far = [move(m, axis, -b) for m, b in zip((message, *blocks[ks][:2]), BACK)]
            blocks[ks] = blocks[ks][2:]
            flying[ks] = far
        else:
            send(ks, message, axis)

    stepped = {}

    def adam(ks):
        own, = blocks[ks]
        came = flying[ks] if isinstance(flying[ks], list) else [flying[ks]]
        stepped[offsets[ks[0]]] = line.call(
            functools.partial(adam_kernel, offsets[ks[0]]), "adam", [(own.shape, f32)],
            *weights, own, *came, scalars=(fix,),
        )[0]

    fetch("a")
    sib_grads = move(out_grads, "core")
    gm = picked(out_grads)
    fetch("b", gm)
    gs = picked(sib_grads)
    fetch("e", gs)
    produce("a", "y")
    fetch("c", blocks["a"][0])
    produce("b", "y")
    fetch("d", blocks["b"][0])
    produce("e", "z")
    relay("a", "y")
    relay("b", "y")
    relay("e", "z")
    relay("a", "y")
    relay("b", "y")
    relay("e", "z")
    produce("c", "y")
    produce("d", "y")
    settle("ab", "z")
    relay("c", "y")
    relay("d", "y")
    settle("e", "y")
    relay("ab", "z")
    relay("c", "y")
    relay("d", "y")
    relay("e", "y")
    relay("ab", "z")
    settle("cd", "z", direct=True)
    relay("e", "y")
    adam("ab")
    adam("e")
    adam("cd")
    stepped = [stepped[k] for k in sorted(stepped)]
    stepped = jnp.concatenate(stepped, axis=1)
    wide = width // workers
    parts = lax.all_to_all(stepped, "worker", split_axis=1, concat_axis=0, tiled=True)
    delta = global_weight - jnp.sum(parts.reshape(workers, share, wide), axis=0) / workers
    momentum = 0.9 * outer_momentum + delta
    updated = global_weight - 0.7 * (delta + 0.9 * momentum)
    piece = updated.astype(bf16)
    spread = jnp.broadcast_to(piece[None], (workers,) + piece.shape).reshape(workers * share, wide)
    synced = lax.all_to_all(spread, "worker", split_axis=0, concat_axis=1, tiled=True)
    return (synced, updated, momentum)


def solution(mesh):
    placed = (
        P(("worker", "shard"), None),
        P(("worker", "shard"), None),
        P("worker", "shard", None),
        P("worker", "shard", None),
        P("worker", "shard", None),
        P("shard", "worker"),
        P("shard", "worker"),
        P(),
    )
    return jax.shard_map(
        local,
        mesh=mesh,
        in_specs=placed,
        out_specs=(P("shard", None), P("shard", "worker"), P("shard", "worker")),
        check_vma=False,
    )
```

time: 277 us -> 165 us (0.60)
  waiting for transfers between devices: 209 us -> 56.7 us
  starting transfers between devices: 0.08 us -> 39.6 us
  Pallas kernels: 0 us -> 16.5 us
  matrix products: 15.8 us -> 0 us
  between operations: 14.8 us -> 1.76 us
  local copies, waits for them, and re-layouts: 1.97 us -> 10.4 us
  blocking collectives: 29.1 us -> 36.8 us
  other arithmetic: 4.67 us -> 1.11 us
    reduce_scatter x2 -> x0, waiting for transfers between devices: 209 us -> none  [the longest x1 168 us: local(): lax.psum_scatter(gradient_term(jnp.int32(0), lax.axis_size('shard') * sha...]
    ppermute x0 -> x30, waiting for transfers between devices: none -> 56.7 us  [move(): return lax.ppermute(array, 'shard', pairs)]
    ppermute x0 -> x30, starting transfers between devices: none -> 39.6 us  [move(): return lax.ppermute(array, 'shard', pairs)]
    all_to_all x0 -> x2, blocking collectives: none -> 36.8 us  [the longest x1 25.3 us: local(): lax.all_to_all(stepped, 'worker', split_axis=1, concat_axis=0, tiled=True)]
    all_gather x1 -> x0, blocking collectives: 29.1 us -> none  [local(): lax.all_gather(updated.astype(jnp.bfloat16), 'worker', axis=1, tiled=True)]
    pallas_call x0 -> x27, Pallas kernels: none -> 16.5 us  [call(): pl.pallas_call(lambda *refs: kernel(*refs[skip:]), out_shape=[jax.ShapeDt...]
    dot_general x1 -> x0, matrix products: 15.8 us -> none  [gradient_term(): lax.dot_general(picked, acts, (((0,), (0,)), ((), ())), preferred_element...]
    slice x0 -> x5, local copies, waits for them, and re-layouts: none -> 7.83 us  [fetch(): lax.slice_in_dim(after(acts, *others), offsets[k], offsets[k] + WIDTHS[k]...]
  transfers between devices with their start and end apart: 2 -> 30, of which waited for: 2 -> 12; matrix products, arithmetic and copies ran while one was open for 0% -> 4% of each run, Pallas kernels for 0% -> 10%
where the time goes in v1:
time: 165 us; the launch traced here: 163 us
  waiting for transfers between devices  56.7 us (34%)
  starting transfers between devices  39.6 us (24%)
  blocking collectives  36.8 us (22%)
  Pallas kernels  16.5 us (10%)
  local copies, waits for them, and re-layouts  10.4 us (6%)
  between operations  1.76 us (1%)
    ppermute x30, waiting for transfers between devices, move(): return lax.ppermute(array, 'shard', pairs)  56.7 us
    ppermute x30, starting transfers between devices, move(): return lax.ppermute(array, 'shard', pairs)  39.6 us
    all_to_all x1, blocking collectives, local(): lax.all_to_all(stepped, 'worker', split_axis=1, concat_axis=0, tiled=True)  25.3 us
    pallas_call x27, Pallas kernels, call(): pl.pallas_call(lambda *refs: kernel(*refs[skip:]), out_shape=[jax.ShapeDt...  16.5 us
    all_to_all x1, blocking collectives, local(): lax.all_to_all(spread, 'worker', split_axis=0, concat_axis=1, tiled=True)  11.4 us
    slice x5, local copies, waits for them, and re-layouts, fetch(): lax.slice_in_dim(after(acts, *others), offsets[k], offsets[k] + WIDTHS[k]...  7.83 us
  transfers between devices with their start and end apart: 30, of which 12 were waited for; matrix products, arithmetic and copies ran while one was open for 4% of the time, Pallas kernels for 10%

profile of v1, /device:TPU:64, one launch (start us, length us, event | category | flops | bytes accessed | tf_op | source)
XLA Modules:
  0.0 162.8 jit_solution(16182518130589085082)
XLA Ops:
  0.6 1.8 %slice.20.refs_3_ = bf16[512,2304]{1,0:T(8,128)(2,1)S(1)} slice(bf16[512,8192]{1,0:T(8,128)(2,1)} %param.9), slice={[0:512], [0:2304]} | slice | bytes 4718592 | tf_op jit(solution)/shard_map/slice | solution.py:155
  5.1 1.9 %slice.16.refs_3_ = bf16[512,2304]{1,0:T(8,128)(2,1)S(1)} slice(bf16[512,8192]{1,0:T(8,128)(2,1)} %param.9), slice={[0:512], [2304:4608]} | slice | bytes 4718592 | tf_op jit(solution)/shard_map/slice | solution.py:155
  7.7 5.6 %collective-permute-done.refs_2_ = bf16[512,1024]{1,0:T(8,128)(2,1)S(1)} collective-permute-done((bf16[512,1024]{1,0:T(8,128)(2,1)S(1)}, bf16[512,1024]{1,0:T(8,128)(2,1)S(1)}, u32[]{:S(2)}, u32[]{:S(2)}) %collective-permute-start) | collective-permute-done | bytes 1048608 | tf_op jit(solution)/shard_map/ppermute | solution.py:39
  16.0 4.3 %product.5 = (bf16[128,2304]{1,0:T(8,128)(2,1)S(1)}, f32[128,2304]{1,0:T(8,128)S(1)}, f32[128,2304]{1,0:T(8,128)S(1)}, f32[128,2304]{1,0:T(8,128)S(1)}) custom-call(bf16[512,512]{1,0:T(8,128)(2,1)S(1)} %pick.3.refs_0_.refs_2_, bf16[512,512]{1,0:T(8,128)(2,1)S(1)} %pick.2.refs_0_.refs_1_, bf16[512,512]{1,0:T(8,128)(2,1)S(1)} %pick.3.refs_0_.refs_2_, ...), custom_call_target="tpu_custom_call" | custom-call | tf_op jit(solution)/shard_map/product/pallas_call | solution.py:52
  21.9 2.6 %product.6 = (bf16[128,2304]{1,0:T(8,128)(2,1)S(1)}, f32[128,2304]{1,0:T(8,128)S(1)}, f32[128,2304]{1,0:T(8,128)S(1)}, f32[128,2304]{1,0:T(8,128)S(1)}) custom-call(bf16[128,2304]{1,0:T(8,128)(2,1)S(1)} %get-tuple-element.39.refs_0_, bf16[512,512]{1,0:T(8,128)(2,1)S(1)} %pick.2.refs_0_.refs_1_, bf16[512,512]{1,0:T(8,128)(2,1)S(1)} %pick.3.refs_0_.refs_2_, ...), custom_call_target="tpu_custom_call" | custom-call | tf_op jit(solution)/shard_map/product/pallas_call | solution.py:52
  24.5 1.7 %collective-permute-start.5 = (bf16[128,2304]{1,0:T(8,128)(2,1)S(1)}, bf16[128,2304]{1,0:T(8,128)(2,1)S(1)}, u32[]{:S(2)}, u32[]{:S(2)}) collective-permute-start(bf16[128,2304]{1,0:T(8,128)(2,1)S(1)} %get-tuple-element.41.refs_0_), channel_id=1, source_target_pairs={{0,2},{1,7},{2,4},{3,1},{4,6},{5,3},{6,0},{7,5},{8,10},{9,15},{10,... | collective-permute-start | bytes 1769480 | tf_op jit(solution)/shard_map/ppermute | solution.py:39
  26.2 1.8 %product.7 = (bf16[128,1536]{1,0:T(8,128)(2,1)S(1)}, f32[128,1536]{1,0:T(8,128)S(1)}, f32[128,1536]{1,0:T(8,128)S(1)}, f32[128,1536]{1,0:T(8,128)S(1)}) custom-call(bf16[128,2304]{1,0:T(8,128)(2,1)S(1)} %get-tuple-element.41.refs_0_, bf16[512,512]{1,0:T(8,128)(2,1)S(1)} %pick.2.refs_0_.refs_1_, bf16[512,512]{1,0:T(8,128)(2,1)S(1)} %pick.3.refs_0_.refs_2_, ...), custom_call_target="tpu_custom_call" | custom-call | tf_op jit(solution)/shard_map/product/pallas_call | solution.py:52
  28.0 3.5 %collective-permute-done.4.refs_2_ = bf16[128,2304]{1,0:T(8,128)(2,1)S(1)} collective-permute-done((bf16[128,2304]{1,0:T(8,128)(2,1)S(1)}, bf16[128,2304]{1,0:T(8,128)(2,1)S(1)}, u32[]{:S(2)}, u32[]{:S(2)}) %collective-permute-start.4) | collective-permute-done | bytes 589856 | tf_op jit(solution)/shard_map/ppermute | solution.py:39
  32.0 5.8 %collective-permute-done.5.refs_2_ = bf16[128,2304]{1,0:T(8,128)(2,1)S(1)} collective-permute-done((bf16[128,2304]{1,0:T(8,128)(2,1)S(1)}, bf16[128,2304]{1,0:T(8,128)(2,1)S(1)}, u32[]{:S(2)}, u32[]{:S(2)}) %collective-permute-start.5) | collective-permute-done | bytes 589856 | tf_op jit(solution)/shard_map/ppermute | solution.py:39
  42.6 4.6 %collective-permute-start.6 = (bf16[128,1536]{1,0:T(8,128)(2,1)S(1)}, bf16[128,1536]{1,0:T(8,128)(2,1)S(1)}, u32[]{:S(2)}, u32[]{:S(2)}) collective-permute-start(bf16[128,1536]{1,0:T(8,128)(2,1)S(1)} %get-tuple-element.43.refs_0_), channel_id=1, source_target_pairs={{0,8},{1,25},{2,10},{3,27},{4,12},{5,29},{6,14},{7,31},{8,16},{9,1... | collective-permute-start | bytes 1179656 | tf_op jit(solution)/shard_map/ppermute | solution.py:39
  47.2 9.4 %collective-permute-done.6.refs_2_ = bf16[128,1536]{1,0:T(8,128)(2,1)S(1)} collective-permute-done((bf16[128,1536]{1,0:T(8,128)(2,1)S(1)}, bf16[128,1536]{1,0:T(8,128)(2,1)S(1)}, u32[]{:S(2)}, u32[]{:S(2)}) %collective-permute-start.6) | collective-permute-done | bytes 393248 | tf_op jit(solution)/shard_map/ppermute | solution.py:39
  58.9 4.6 %collective-permute-start.9 = (bf16[128,1536]{1,0:T(8,128)(2,1)S(1)}, bf16[128,1536]{1,0:T(8,128)(2,1)S(1)}, u32[]{:S(2)}, u32[]{:S(2)}) collective-permute-start(bf16[128,1536]{1,0:T(8,128)(2,1)S(1)} %relay.16.refs_0_), channel_id=1, source_target_pairs={{0,8},{1,25},{2,10},{3,27},{4,12},{5,29},{6,14},{7,31},{8,16},{9,1... | collective-permute-start | bytes 1179656 | tf_op jit(solution)/shard_map/ppermute | solution.py:39
  63.5 8.4 %collective-permute-done.9.refs_2_ = bf16[128,1536]{1,0:T(8,128)(2,1)S(1)} collective-permute-done((bf16[128,1536]{1,0:T(8,128)(2,1)S(1)}, bf16[128,1536]{1,0:T(8,128)(2,1)S(1)}, u32[]{:S(2)}, u32[]{:S(2)}) %collective-permute-start.9) | collective-permute-done | bytes 393248 | tf_op jit(solution)/shard_map/ppermute | solution.py:39
  72.0 4.7 %collective-permute-start.16 = (bf16[128,1536]{1,0:T(8,128)(2,1)S(1)}, bf16[128,1536]{1,0:T(8,128)(2,1)S(1)}, u32[]{:S(2)}, u32[]{:S(2)}) collective-permute-start(bf16[128,1536]{1,0:T(8,128)(2,1)S(1)} %relay.19.refs_0_), channel_id=1, source_target_pairs={{0,8},{1,25},{2,10},{3,27},{4,12},{5,29},{6,14},{7,31},{8,16},{9,1... | collective-permute-start | bytes 1179656 | tf_op jit(solution)/shard_map/ppermute | solution.py:39
  82.6 2.9 %collective-permute-done.14.refs_2_ = bf16[128,1024]{1,0:T(8,128)(2,1)S(1)} collective-permute-done((bf16[128,1024]{1,0:T(8,128)(2,1)S(1)}, bf16[128,1024]{1,0:T(8,128)(2,1)S(1)}, u32[]{:S(2)}, u32[]{:S(2)}) %collective-permute-start.14) | collective-permute-done | bytes 262176 | tf_op jit(solution)/shard_map/ppermute | solution.py:39
  85.9 2.5 %collective-permute-done.15.refs_2_ = bf16[128,1024]{1,0:T(8,128)(2,1)S(1)} collective-permute-done((bf16[128,1024]{1,0:T(8,128)(2,1)S(1)}, bf16[128,1024]{1,0:T(8,128)(2,1)S(1)}, u32[]{:S(2)}, u32[]{:S(2)}) %collective-permute-start.15) | collective-permute-done | bytes 262176 | tf_op jit(solution)/shard_map/ppermute | solution.py:39
  88.8 5.4 %collective-permute-done.17.refs_2_ = bf16[32,4608]{1,0:T(8,128)(2,1)S(1)} collective-permute-done((bf16[32,4608]{1,0:T(8,128)(2,1)S(1)}, bf16[32,4608]{1,0:T(8,128)(2,1)S(1)}, u32[]{:S(2)}, u32[]{:S(2)}) %collective-permute-start.17) | collective-permute-done | bytes 294944 | tf_op jit(solution)/shard_map/ppermute | solution.py:39
  99.2 2.3 %collective-permute-done.20.refs_2_ = bf16[32,1536]{1,0:T(8,128)(2,1)S(1)} collective-permute-done((bf16[32,1536]{1,0:T(8,128)(2,1)S(1)}, bf16[32,1536]{1,0:T(8,128)(2,1)S(1)}, u32[]{:S(2)}, u32[]{:S(2)}) %collective-permute-start.20) | collective-permute-done | bytes 98336 | tf_op jit(solution)/shard_map/ppermute | solution.py:39
  101.5 6.3 %collective-permute-done.21.refs_2_ = bf16[32,4608]{1,0:T(8,128)(2,1)S(1)} collective-permute-done((bf16[32,4608]{1,0:T(8,128)(2,1)S(1)}, bf16[32,4608]{1,0:T(8,128)(2,1)S(1)}, u32[]{:S(2)}, u32[]{:S(2)}) %collective-permute-start.21) | collective-permute-done | bytes 294944 | tf_op jit(solution)/shard_map/ppermute | solution.py:39
  108.7 2.4 %collective-permute-start.27 = (bf16[32,2048]{1,0:T(8,128)(2,1)S(1)}, bf16[32,2048]{1,0:T(8,128)(2,1)S(1)}, u32[]{:S(2)}, u32[]{:S(2)}) collective-permute-start(bf16[32,2048]{1,0:T(8,128)(2,1)S(1)} %get-tuple-element.68.refs_0_), channel_id=1, source_target_pairs={{0,24},{1,9},{2,26},{3,11},{4,28},{5,13},{6,30},{7,15},{8,0},{9,17... | collective-permute-start | bytes 393224 | tf_op jit(solution)/shard_map/ppermute | solution.py:39
  111.8 4.0 %collective-permute-start.29 = (bf16[32,2048]{1,0:T(8,128)(2,1)S(1)}, bf16[32,2048]{1,0:T(8,128)(2,1)S(1)}, u32[]{:S(2)}, u32[]{:S(2)}) collective-permute-start(bf16[32,2048]{1,0:T(8,128)(2,1)S(1)} %get-tuple-element.74), channel_id=1, source_target_pairs={{0,8},{1,25},{2,10},{3,27},{4,12},{5,29},{6,14},{7,31},{8,16},{9,1... | collective-permute-start | bytes 393224 | tf_op jit(solution)/shard_map/ppermute | solution.py:39
  118.2 4.3 %collective-permute-done.26.refs_6_ = bf16[32,1536]{1,0:T(8,128)(2,1)S(1)} collective-permute-done((bf16[32,1536]{1,0:T(8,128)(2,1)S(1)}, bf16[32,1536]{1,0:T(8,128)(2,1)S(1)}, u32[]{:S(2)}, u32[]{:S(2)}) %collective-permute-start.26) | collective-permute-done | bytes 98336 | tf_op jit(solution)/shard_map/ppermute | solution.py:39
  124.3 25.3 %all_to_all.29 = f32[32,8,1024]{2,0,1:T(8,128)S(1)} all-to-all(f32[32,8,1024]{2,0,1:T(8,128)S(1)} %bitcast.20), channel_id=1, replica_groups=mesh['worker'=8,'shard'=32] {'worker'}, dimensions={1} | all-to-all | bytes 2097152 | tf_op jit(solution)/shard_map/all_to_all | solution.py:233
  150.5 11.4 %all_to_all.30 = bf16[8,32,1024]{2,1,0:T(8,128)(2,1)S(1)} all-to-all(bf16[8,32,1024]{2,1,0:T(8,128)(2,1)S(1)} %broadcast_in_dim.2), channel_id=1, replica_groups=mesh['worker'=8,'shard'=32] {'worker'}, dimensions={0} | all-to-all | bytes 1048576 | tf_op jit(solution)/shard_map/all_to_all | solution.py:239
  (98 shorter events, 33.7 us)
Async XLA Ops:
  2.5 13.5 %collective-permute-start.1 = (bf16[512,2304]{1,0:T(8,128)(2,1)S(1)}, bf16[512,2304]{1,0:T(8,128)(2,1)}, u32[]{:S(2)}, u32[]{:S(2)}) collective-permute-start(bf16[512,2304]{1,0:T(8,128)(2,1)S(1)} %slice.20.refs_3_), channel_id=1, source_target_pairs={{0,1},{1,0},{2,3},{3,2},{4,5},{5,4},{6,7},{7,6},{8,9},{9,8},{10,11... | collective-permute-start | bytes 7077896 | tf_op jit(solution)/shard_map/ppermute | solution.py:39
  7.1 14.8 %collective-permute-start.2 = (bf16[512,2304]{1,0:T(8,128)(2,1)S(1)}, bf16[512,2304]{1,0:T(8,128)(2,1)S(1)}, u32[]{:S(2)}, u32[]{:S(2)}) collective-permute-start(bf16[512,2304]{1,0:T(8,128)(2,1)S(1)} %slice.16.refs_3_), channel_id=1, source_target_pairs={{0,1},{1,0},{2,3},{3,2},{4,5},{5,4},{6,7},{7,6},{8,9},{9,8},{10,11... | collective-permute-start | bytes 7077896 | tf_op jit(solution)/shard_map/ppermute | solution.py:39
  15.5 10.7 %collective-permute-start.3 = (bf16[512,1536]{1,0:T(8,128)(2,1)S(1)}, bf16[512,1536]{1,0:T(8,128)(2,1)S(1)}, u32[]{:S(2)}, u32[]{:S(2)}) collective-permute-start(bf16[512,1536]{1,0:T(8,128)(2,1)S(1)} %slice.17.refs_3_), channel_id=1, source_target_pairs={{0,1},{1,0},{2,3},{3,2},{4,5},{5,4},{6,7},{7,6},{8,9},{9,8},{10,11... | collective-permute-start | bytes 4718600 | tf_op jit(solution)/shard_map/ppermute | solution.py:39
  20.2 11.2 %collective-permute-start.4 = (bf16[128,2304]{1,0:T(8,128)(2,1)S(1)}, bf16[128,2304]{1,0:T(8,128)(2,1)S(1)}, u32[]{:S(2)}, u32[]{:S(2)}) collective-permute-start(bf16[128,2304]{1,0:T(8,128)(2,1)S(1)} %get-tuple-element.39.refs_0_), channel_id=1, source_target_pairs={{0,2},{1,7},{2,4},{3,1},{4,6},{5,3},{6,0},{7,5},{8,10},{9,15},{10,... | collective-permute-start | bytes 1769480 | tf_op jit(solution)/shard_map/ppermute | solution.py:39
  24.5 13.2 %collective-permute-start.5 = (bf16[128,2304]{1,0:T(8,128)(2,1)S(1)}, bf16[128,2304]{1,0:T(8,128)(2,1)S(1)}, u32[]{:S(2)}, u32[]{:S(2)}) collective-permute-start(bf16[128,2304]{1,0:T(8,128)(2,1)S(1)} %get-tuple-element.41.refs_0_), channel_id=1, source_target_pairs={{0,2},{1,7},{2,4},{3,1},{4,6},{5,3},{6,0},{7,5},{8,10},{9,15},{10,... | collective-permute-start | bytes 1769480 | tf_op jit(solution)/shard_map/ppermute | solution.py:39
  31.5 25.1 %collective-permute-start.7 = (bf16[128,2304]{1,0:T(8,128)(2,1)S(1)}, bf16[128,2304]{1,0:T(8,128)(2,1)S(1)}, u32[]{:S(2)}, u32[]{:S(2)}) collective-permute-start(bf16[128,2304]{1,0:T(8,128)(2,1)S(1)} %relay.14.refs_0_), channel_id=1, source_target_pairs={{0,2},{1,7},{2,4},{3,1},{4,6},{5,3},{6,0},{7,5},{8,10},{9,15},{10,... | collective-permute-start | bytes 1769480 | tf_op jit(solution)/shard_map/ppermute | solution.py:39
  37.8 18.9 %collective-permute-start.8 = (bf16[128,2304]{1,0:T(8,128)(2,1)S(1)}, bf16[128,2304]{1,0:T(8,128)(2,1)S(1)}, u32[]{:S(2)}, u32[]{:S(2)}) collective-permute-start(bf16[128,2304]{1,0:T(8,128)(2,1)S(1)} %relay.15.refs_0_), channel_id=1, source_target_pairs={{0,2},{1,7},{2,4},{3,1},{4,6},{5,3},{6,0},{7,5},{8,10},{9,15},{10,... | collective-permute-start | bytes 1769480 | tf_op jit(solution)/shard_map/ppermute | solution.py:39
  39.6 37.0 %collective-permute-start.10 = (bf16[512,1024]{1,0:T(8,128)(2,1)S(1)}, bf16[512,1024]{1,0:T(8,128)(2,1)S(1)}, u32[]{:S(2)}, u32[]{:S(2)}) collective-permute-start(bf16[512,1024]{1,0:T(8,128)(2,1)S(1)} %slice.18.refs_3_), channel_id=1, source_target_pairs={{0,1},{1,0},{2,3},{3,2},{4,5},{5,4},{6,7},{7,6},{8,9},{9,8},{10,11... | collective-permute-start | bytes 3145736 | tf_op jit(solution)/shard_map/ppermute | solution.py:39
  42.5 36.9 %collective-permute-start.11 = (bf16[512,1024]{1,0:T(8,128)(2,1)S(1)}, bf16[512,1024]{1,0:T(8,128)(2,1)S(1)}, u32[]{:S(2)}, u32[]{:S(2)}) collective-permute-start(bf16[512,1024]{1,0:T(8,128)(2,1)S(1)} %slice.19.refs_3_), channel_id=1, source_target_pairs={{0,1},{1,0},{2,3},{3,2},{4,5},{5,4},{6,7},{7,6},{8,9},{9,8},{10,11... | collective-permute-start | bytes 3145736 | tf_op jit(solution)/shard_map/ppermute | solution.py:39
  42.6 14.0 %collective-permute-start.6 = (bf16[128,1536]{1,0:T(8,128)(2,1)S(1)}, bf16[128,1536]{1,0:T(8,128)(2,1)S(1)}, u32[]{:S(2)}, u32[]{:S(2)}) collective-permute-start(bf16[128,1536]{1,0:T(8,128)(2,1)S(1)} %get-tuple-element.43.refs_0_), channel_id=1, source_target_pairs={{0,8},{1,25},{2,10},{3,27},{4,12},{5,29},{6,14},{7,31},{8,16},{9,1... | collective-permute-start | bytes 1179656 | tf_op jit(solution)/shard_map/ppermute | solution.py:39
  56.9 25.1 %collective-permute-start.13 = (bf16[128,2304]{1,0:T(8,128)(2,1)S(1)}, bf16[128,2304]{1,0:T(8,128)(2,1)S(1)}, u32[]{:S(2)}, u32[]{:S(2)}) collective-permute-start(bf16[128,2304]{1,0:T(8,128)(2,1)S(1)} %relay.18.refs_0_), channel_id=1, source_target_pairs={{0,2},{1,7},{2,4},{3,1},{4,6},{5,3},{6,0},{7,5},{8,10},{9,15},{10,... | collective-permute-start | bytes 1769480 | tf_op jit(solution)/shard_map/ppermute | solution.py:39
  57.6 24.4 %collective-permute-start.12 = (bf16[128,2304]{1,0:T(8,128)(2,1)S(1)}, bf16[128,2304]{1,0:T(8,128)(2,1)S(1)}, u32[]{:S(2)}, u32[]{:S(2)}) collective-permute-start(bf16[128,2304]{1,0:T(8,128)(2,1)S(1)} %relay.17.refs_0_), channel_id=1, source_target_pairs={{0,2},{1,7},{2,4},{3,1},{4,6},{5,3},{6,0},{7,5},{8,10},{9,15},{10,... | collective-permute-start | bytes 1769480 | tf_op jit(solution)/shard_map/ppermute | solution.py:39
  58.9 13.0 %collective-permute-start.9 = (bf16[128,1536]{1,0:T(8,128)(2,1)S(1)}, bf16[128,1536]{1,0:T(8,128)(2,1)S(1)}, u32[]{:S(2)}, u32[]{:S(2)}) collective-permute-start(bf16[128,1536]{1,0:T(8,128)(2,1)S(1)} %relay.16.refs_0_), channel_id=1, source_target_pairs={{0,8},{1,25},{2,10},{3,27},{4,12},{5,29},{6,14},{7,31},{8,16},{9,1... | collective-permute-start | bytes 1179656 | tf_op jit(solution)/shard_map/ppermute | solution.py:39
  72.0 16.7 %collective-permute-start.16 = (bf16[128,1536]{1,0:T(8,128)(2,1)S(1)}, bf16[128,1536]{1,0:T(8,128)(2,1)S(1)}, u32[]{:S(2)}, u32[]{:S(2)}) collective-permute-start(bf16[128,1536]{1,0:T(8,128)(2,1)S(1)} %relay.19.refs_0_), channel_id=1, source_target_pairs={{0,8},{1,25},{2,10},{3,27},{4,12},{5,29},{6,14},{7,31},{8,16},{9,1... | collective-permute-start | bytes 1179656 | tf_op jit(solution)/shard_map/ppermute | solution.py:39
  82.2 11.9 %collective-permute-start.17 = (bf16[32,4608]{1,0:T(8,128)(2,1)S(1)}, bf16[32,4608]{1,0:T(8,128)(2,1)S(1)}, u32[]{:S(2)}, u32[]{:S(2)}) collective-permute-start(bf16[32,4608]{1,0:T(8,128)(2,1)S(1)} %get-tuple-element.56.refs_0_), channel_id=1, source_target_pairs={{0,8},{1,25},{2,10},{3,27},{4,12},{5,29},{6,14},{7,31},{8,16},{9,1... | collective-permute-start | bytes 884744 | tf_op jit(solution)/shard_map/ppermute | solution.py:39
  85.6 11.5 %collective-permute-start.18 = (bf16[128,1024]{1,0:T(8,128)(2,1)S(1)}, bf16[128,1024]{1,0:T(8,128)(2,1)S(1)}, u32[]{:S(2)}, u32[]{:S(2)}) collective-permute-start(bf16[128,1024]{1,0:T(8,128)(2,1)S(1)} %relay.20.refs_0_), channel_id=1, source_target_pairs={{0,2},{1,7},{2,4},{3,1},{4,6},{5,3},{6,0},{7,5},{8,10},{9,15},{10,... | collective-permute-start | bytes 786440 | tf_op jit(solution)/shard_map/ppermute | solution.py:39
  88.4 8.7 %collective-permute-start.19 = (bf16[128,1024]{1,0:T(8,128)(2,1)S(1)}, bf16[128,1024]{1,0:T(8,128)(2,1)S(1)}, u32[]{:S(2)}, u32[]{:S(2)}) collective-permute-start(bf16[128,1024]{1,0:T(8,128)(2,1)S(1)} %relay.21.refs_0_), channel_id=1, source_target_pairs={{0,2},{1,7},{2,4},{3,1},{4,6},{5,3},{6,0},{7,5},{8,10},{9,15},{10,... | collective-permute-start | bytes 786440 | tf_op jit(solution)/shard_map/ppermute | solution.py:39
  94.2 13.6 %collective-permute-start.21 = (bf16[32,4608]{1,0:T(8,128)(2,1)S(1)}, bf16[32,4608]{1,0:T(8,128)(2,1)S(1)}, u32[]{:S(2)}, u32[]{:S(2)}) collective-permute-start(bf16[32,4608]{1,0:T(8,128)(2,1)S(1)} %relay.22.refs_0_), channel_id=1, source_target_pairs={{0,8},{1,25},{2,10},{3,27},{4,12},{5,29},{6,14},{7,31},{8,16},{9,1... | collective-permute-start | bytes 884744 | tf_op jit(solution)/shard_map/ppermute | solution.py:39
  97.2 11.4 %collective-permute-start.23 = (bf16[128,1024]{1,0:T(8,128)(2,1)S(1)}, bf16[128,1024]{1,0:T(8,128)(2,1)S(1)}, u32[]{:S(2)}, u32[]{:S(2)}) collective-permute-start(bf16[128,1024]{1,0:T(8,128)(2,1)S(1)} %relay.24.refs_0_), channel_id=1, source_target_pairs={{0,2},{1,7},{2,4},{3,1},{4,6},{5,3},{6,0},{7,5},{8,10},{9,15},{10,... | collective-permute-start | bytes 786440 | tf_op jit(solution)/shard_map/ppermute | solution.py:39
  98.6 10.0 %collective-permute-start.22 = (bf16[128,1024]{1,0:T(8,128)(2,1)S(1)}, bf16[128,1024]{1,0:T(8,128)(2,1)S(1)}, u32[]{:S(2)}, u32[]{:S(2)}) collective-permute-start(bf16[128,1024]{1,0:T(8,128)(2,1)S(1)} %relay.23.refs_0_), channel_id=1, source_target_pairs={{0,2},{1,7},{2,4},{3,1},{4,6},{5,3},{6,0},{7,5},{8,10},{9,15},{10,... | collective-permute-start | bytes 786440 | tf_op jit(solution)/shard_map/ppermute | solution.py:39
  107.9 9.2 %collective-permute-start.25 = (bf16[32,4608]{1,0:T(8,128)(2,1)S(1)}, bf16[32,4608]{1,0:T(8,128)(2,1)S(1)}, u32[]{:S(2)}, u32[]{:S(2)}) collective-permute-start(bf16[32,4608]{1,0:T(8,128)(2,1)S(1)} %relay.26.refs_0_), channel_id=1, source_target_pairs={{0,8},{1,25},{2,10},{3,27},{4,12},{5,29},{6,14},{7,31},{8,16},{9,1... | collective-permute-start | bytes 884744 | tf_op jit(solution)/shard_map/ppermute | solution.py:39
  108.7 14.6 %collective-permute-start.27 = (bf16[32,2048]{1,0:T(8,128)(2,1)S(1)}, bf16[32,2048]{1,0:T(8,128)(2,1)S(1)}, u32[]{:S(2)}, u32[]{:S(2)}) collective-permute-start(bf16[32,2048]{1,0:T(8,128)(2,1)S(1)} %get-tuple-element.68.refs_0_), channel_id=1, source_target_pairs={{0,24},{1,9},{2,26},{3,11},{4,28},{5,13},{6,30},{7,15},{8,0},{9,17... | collective-permute-start | bytes 393224 | tf_op jit(solution)/shard_map/ppermute | solution.py:39
  111.1 12.2 %collective-permute-start.28 = (bf16[32,2048]{1,0:T(8,128)(2,1)S(1)}, bf16[32,2048]{1,0:T(8,128)(2,1)S(1)}, u32[]{:S(2)}, u32[]{:S(2)}) collective-permute-start(bf16[32,2048]{1,0:T(8,128)(2,1)S(1)} %get-tuple-element.73), channel_id=1, source_target_pairs={{0,16},{1,17},{2,18},{3,19},{4,20},{5,21},{6,22},{7,23},{8,24},{9,... | collective-permute-start | bytes 393224 | tf_op jit(solution)/shard_map/ppermute | solution.py:39
  111.8 11.5 %collective-permute-start.29 = (bf16[32,2048]{1,0:T(8,128)(2,1)S(1)}, bf16[32,2048]{1,0:T(8,128)(2,1)S(1)}, u32[]{:S(2)}, u32[]{:S(2)}) collective-permute-start(bf16[32,2048]{1,0:T(8,128)(2,1)S(1)} %get-tuple-element.74), channel_id=1, source_target_pairs={{0,8},{1,25},{2,10},{3,27},{4,12},{5,29},{6,14},{7,31},{8,16},{9,1... | collective-permute-start | bytes 393224 | tf_op jit(solution)/shard_map/ppermute | solution.py:39
  (14 other events, 125.7 us)

commit v2 on v0

v2 whole, which is shorter than its diff:
```python
import functools
import math

import jax
import jax.numpy as jnp
from jax import lax
from jax.experimental import pallas as pl
from jax.experimental.pallas import tpu as pltpu
from jax.sharding import PartitionSpec as P

WIDTHS = {"a": 2048, "b": 2048, "e": 1536, "c": 1536, "d": 1024}
TILE = 512


NZ, NY, NC = 4, 4, 2
SHARDS = NZ * NY * NC
BACK = (1, 2, 3, 0)
VMEM = pl.BlockSpec(memory_space=pltpu.VMEM)
ANY = pl.BlockSpec(memory_space=pl.ANY)
LIMIT = 12 << 20
COST = {"product": 50_000_000_000, "pick": 50_000_000_000}
OTHER_COST = 2_000_000_000
LATE_COST = 500_000_000
bf16, f32 = jnp.bfloat16, jnp.float32


def shard_of(z, y, c):
    return (z % NZ * NY + y % NY) * NC + c % NC


def sense(c):
    return 1 if c == 0 else -1


def move(array, axis, steps=1):
    pairs = []
    for z in range(NZ):
        for y in range(NY):
            for c in range(NC):
                by = steps * sense(c)
                to = {
                    "z": shard_of(z + by, y, c), "y": shard_of(z, y + by, c), "core": shard_of(z, y, c + 1)
                }[axis]
                pairs.append((shard_of(z, y, c), to))
    return lax.ppermute(array, "shard", pairs)


class Line:
    def __init__(self):
        self.last = None

    def call(self, name, *parts, scalars=(), **more):
        before = () if self.last is None else (self.last,)
        lead = len(before) + len(scalars)
        outs = [o for _, out, _ in parts for o in out]
        operands = [o for _, _, ins in parts for o in ins]

        def body(*refs):
            given, made, scratch = lead, lead + len(operands), refs[lead + len(operands) + len(outs):]
            for kernel, out, ins in parts:
                kernel(
                    *refs[len(before):lead], *refs[given:given + len(ins)], *refs[made:made + len(out)], *scratch
                )
                given, made = given + len(ins), made + len(out)

        flops = more.get("cost", COST.get(name, OTHER_COST))
        results = pl.pallas_call(
            body,
            out_shape=[jax.ShapeDtypeStruct(s, t) for s, t in outs],
            in_specs=[ANY] * len(before)
            + [pl.BlockSpec(memory_space=pltpu.SMEM)] * len(scalars)
            + (more.get("specs") or [VMEM] * len(operands)),
            out_specs=more.get("out_specs") or [VMEM] * len(outs),
            scratch_shapes=more.get("scratch", ()),
            grid=more.get("grid", ()),
            compiler_params=pltpu.CompilerParams(vmem_limit_bytes=more.get("limit", LIMIT)),
            cost_estimate=pl.CostEstimate(flops=flops, bytes_accessed=flops // 100, transcendentals=0),
            name=name,
        )(*before, *scalars, *operands)
        self.last = results[0]
        split, at = [], 0
        for _, out, _ in parts:
            split.append(results[at:at + len(out)])
            at += len(out)
        return split


def pick_kernel(share, factor, grads_ref, *outs):
    index = lax.axis_index("shard")
    y, z = (index // NC) % NY, index // (NC * NY)
    for out_ref, core in zip(outs, (index % NC, 1 - index % NC)):
        way = 1 - 2 * core
        row = lax.broadcasted_iota(jnp.int32, (out_ref.shape[0], 1), 0)
        block = row // share
        back_y, back_z = (block // NZ + 1) % NY, (block % NZ + 1) % NZ
        owner = ((z + NZ - way * back_z) % NZ * NY + (y + NY - way * back_y) % NY) * NC + core
        feature = owner * share + row % share
        place = lax.broadcasted_iota(jnp.int32, (out_ref.shape[0], grads_ref.shape[1]), 1)
        pick = jnp.where(feature == place, factor, 0.0).astype(bf16)
        out_ref[...] = lax.dot_general(
            pick, grads_ref[...], (((1,), (1,)), ((), ())), preferred_element_type=f32
        ).astype(bf16)


def product_kernel(split, first, mine_rows, sib_rows, acts_ref, mine_ref, sib_ref, held, sems):
    copies = [
        pltpu.make_async_copy(acts_ref.at[:, pl.ds(first + i * TILE, TILE)], held.at[i], sems.at[i])
        for i in range(held.shape[0])
    ]
    for copy in copies:
        copy.start()
    for i, copy in enumerate(copies):
        copy.wait()
        for start in range(0, TILE, TILE // 2):
            tile = held[i, :, start:start + TILE // 2]
            for rows_ref, out in ((sib_rows, sib_ref), (mine_rows, mine_ref)):
                total = jnp.dot(rows_ref[...], tile, preferred_element_type=f32).astype(bf16)
                at = pl.ds(i * TILE + start, TILE // 2)
                out[:, at] = jnp.concatenate([total[r] for rows in split for r in rows], axis=0)


def sum_of(at, terms):
    total = 0.0
    for ref, whole in terms:
        total += (ref[...] if whole else ref[at]).astype(f32)
    return total


def relay_kernel(at, wholes, *refs):
    refs[-1][...] = sum_of(at, zip(refs, wholes)).astype(bf16)


def settle_kernel(at, wholes, n, *refs):
    each = len(wholes)
    outs = refs[each * n:]
    start = 0
    for i in range(n):
        ins = refs[each * i:each * (i + 1)]
        part = slice(start, start + ins[0].shape[1])
        start += ins[0].shape[1]
        total = sum_of(at, zip(ins, wholes))
        row = 0
        for out in outs:
            out[:, part] = total[row:row + out.shape[0]].astype(out.dtype)
            row += out.shape[0]


def adam_kernel(start, fix_ref, weight_ref, mean_ref, var_ref, own_ref, *refs):
    came, out_ref = refs[:-1], refs[-1]
    at = pl.ds(start, own_ref.shape[1])
    grad = own_ref[own_ref.shape[0] - out_ref.shape[0]:].astype(f32)
    for ref in came:
        grad += ref[...].astype(f32)
    weight = weight_ref[:, at].astype(f32)
    moment = 0.9 * mean_ref[:, at] + 0.1 * grad
    second = 0.95 * var_ref[:, at] + 0.05 * grad * grad
    ratio = moment / fix_ref[0] / (jnp.sqrt(second / fix_ref[1]) + 1e-08)
    out_ref[...] = weight - 0.1 * (ratio + 0.1 * weight)


def local(acts, out_grads, local_weight, adam_mean, adam_var, global_weight, outer_momentum, step_count):
    workers = lax.axis_size("worker")
    tokens, width = acts.shape
    features = out_grads.shape[1]
    share = features // SHARDS
    half = features // NC
    rows = half // NY
    factor = 1.0 / math.sqrt(tokens * SHARDS)
    count = step_count[0].astype(f32)
    offsets, total = {}, 0
    for k, cols in WIDTHS.items():
        offsets[k] = total
        total += cols

    fix = jnp.stack([1.0 - jnp.power(0.9, count), 1.0 - jnp.power(0.95, count)])
    line = Line()

    blocks, sent, flying = {}, {}, {}
    weights = (local_weight[0], adam_mean[0], adam_var[0])
    by_y = [[slice(i * rows, (i + 1) * rows)] for i in range(NY)]
    by_z = [[slice((j * NZ + i) * share, (j * NZ + i + 1) * share) for j in range(NY)] for i in range(NZ)]

    def produce(k):
        kernel = functools.partial(product_kernel, by_z if k == "e" else by_y, offsets[k])
        tiles = WIDTHS[k] // TILE
        (made, other), = line.call(
            "product", (kernel, [((half, WIDTHS[k]), bf16)] * 2, (mine_rows, sib_rows, acts)), specs=[VMEM, VMEM, ANY],
            scratch=[pltpu.VMEM((tiles, tokens, TILE), bf16), pltpu.SemaphoreType.DMA((tiles,))],
        )
        blocks[k], sent[k], flying[k] = [made, move(other, "core")], 0, None

    def terms(k):
        size = {half: rows, 3 * share: share}[blocks[k][0].shape[0]]
        at = slice(sent[k] * size, (sent[k] + 1) * size)
        came = [] if flying[k] is None else [flying[k]]
        return at, [False] * len(blocks[k]) + [True] * len(came), [*blocks[k], *came]

    def relay(k, axis):
        at, wholes, ins = terms(k)
        shape = at.stop - at.start, ins[0].shape[1]

        def done(made):
            flying[k] = move(made[0], axis)
            sent[k] += 1

        return functools.partial(relay_kernel, at, wholes), [(shape, bf16)], ins, done

    def settle(ks, axis, direct=False):
        cols = sum(WIDTHS[k] for k in ks)
        at, wholes, _ = terms(ks[0])
        ins = [a for k in ks for a in terms(k)[2]]
        if direct:
            out = [((share, cols), bf16)] * 3 + [((share, cols), f32)]
        else:
            out = [((share, cols), bf16), ((3 * share, cols), bf16)]

        def done(made):
            if direct:
                flying[ks] = [move(m, axis, -b) for m, b in zip(made, BACK[:3])]
                blocks[ks], sent[ks] = [made[3]], None
            else:
                flying[ks], blocks[ks], sent[ks] = move(made[0], axis), [made[1]], 0

        return functools.partial(settle_kernel, at, wholes, len(ks)), out, ins, done

    stepped = {}

    def adam(ks):
        start, cols = offsets[ks[0]], sum(WIDTHS[k] for k in ks)
        came = flying[ks] if sent[ks] is None else [flying[ks]]
        last = functools.partial(adam_kernel, start)

        def done(made):
            stepped[start] = made[0]

        return last, [((share, cols), f32)], (*weights, blocks[ks][0], *came), done

    def run(name, *parts, **more):
        results = line.call(name, *[p[:3] for p in parts], **more)
        for made, part in zip(results, parts):
            part[3](made)
        return results[-1]

    (mine_rows, sib_rows), = line.call(
        "pick", (functools.partial(pick_kernel, share, factor), [((half, tokens), bf16)] * 2, (out_grads,))
    )
    produce("a")
    produce("b")
    run("relay", relay("a", "y"))
    produce("e")
    run("relay", relay("b", "y"))
    run("relay", relay("e", "z"))
    produce("c")
    produce("d")
    run("relay", relay("a", "y"))
    run("relay", relay("b", "y"))
    run("relay", relay("e", "z"))
    run("relay", relay("a", "y"))
    run("relay", relay("b", "y"))
    run("relay", relay("c", "y"))
    run("relay", relay("e", "z"))
    run("relay", relay("d", "y"))
    run("settle", settle("ab", "z"))
    run("relay", relay("c", "y"))
    run("relay", relay("d", "y"))
    run("settle", settle("e", "y"))
    run("relay", relay("ab", "z"))
    run("relay", relay("c", "y"), cost=LATE_COST)
    run("relay", relay("e", "y"), cost=LATE_COST)
    run("relay", relay("d", "y"), cost=LATE_COST)
    run("relay", relay("ab", "z"), cost=LATE_COST)
    run("settle", settle("cd", "z", direct=True), cost=LATE_COST)
    run("relay", relay("e", "y"), cost=LATE_COST)
    run("adam", adam("ab"), scalars=(fix,))
    run("adam", adam("e"), scalars=(fix,))
    run("adam", adam("cd"), scalars=(fix,))
    stepped = [stepped[k] for k in sorted(stepped)]
    stepped = jnp.concatenate(stepped, axis=1)
    wide = width // workers
    parts = lax.all_to_all(stepped, "worker", split_axis=1, concat_axis=0, tiled=True)
    delta = global_weight - jnp.sum(parts.reshape(workers, share, wide), axis=0) / workers
    momentum = 0.9 * outer_momentum + delta
    updated = global_weight - 0.7 * (delta + 0.9 * momentum)
    piece = updated.astype(bf16)
    spread = jnp.broadcast_to(piece[None], (workers,) + piece.shape).reshape(workers * share, wide)
    synced = lax.all_to_all(spread, "worker", split_axis=0, concat_axis=1, tiled=True)
    return (synced, updated, momentum)


def solution(mesh):
    placed = (
        P(("worker", "shard"), None),
        P(("worker", "shard"), None),
        P("worker", "shard", None),
        P("worker", "shard", None),
        P("worker", "shard", None),
        P("shard", "worker"),
        P("shard", "worker"),
        P(),
    )
    return jax.shard_map(
        local,
        mesh=mesh,
        in_specs=placed,
        out_specs=(P("shard", None), P("shard", "worker"), P("shard", "worker")),
        check_vma=False,
    )
```

time: 277 us -> 141 us (0.51)
  waiting for transfers between devices: 209 us -> 36.2 us
  starting transfers between devices: 0.08 us -> 45.1 us
  Pallas kernels: 0 us -> 20.2 us
  matrix products: 15.8 us -> 0 us
  between operations: 14.8 us -> 1.68 us
  other arithmetic: 4.67 us -> 0.94 us
  blocking collectives: 29.1 us -> 32.2 us
    reduce_scatter x2 -> x0, waiting for transfers between devices: 209 us -> none  [the longest x1 168 us: local(): lax.psum_scatter(gradient_term(jnp.int32(0), lax.axis_size('shard') * sha...]
    ppermute x0 -> x29, starting transfers between devices: none -> 45.1 us  [move(): return lax.ppermute(array, 'shard', pairs)]
    ppermute x0 -> x29, waiting for transfers between devices: none -> 36.2 us  [move(): return lax.ppermute(array, 'shard', pairs)]
    all_to_all x0 -> x2, blocking collectives: none -> 32.2 us  [the longest x1 20 us: local(): lax.all_to_all(stepped, 'worker', split_axis=1, concat_axis=0, tiled=True)]
    all_gather x1 -> x0, blocking collectives: 29.1 us -> none  [local(): lax.all_gather(updated.astype(jnp.bfloat16), 'worker', axis=1, tiled=True)]
    pallas_call x0 -> x31, Pallas kernels: none -> 20.2 us  [call(): pl.pallas_call(body, out_shape=[jax.ShapeDtypeStruct(s, t) for s, t in ou...]
    dot_general x1 -> x0, matrix products: 15.8 us -> none  [gradient_term(): lax.dot_general(picked, acts, (((0,), (0,)), ((), ())), preferred_element...]
    sub x1 -> x0, other arithmetic: 3.03 us -> none  [inner_step(): return weight - 0.1 * (ratio + 0.1 * weight)]
  transfers between devices with their start and end apart: 2 -> 29, of which waited for: 2 -> 15; matrix products, arithmetic and copies ran while one was open for 0% -> 0% of each run, Pallas kernels for 0% -> 10%
where the time goes in v2:
time: 141 us
  starting transfers between devices  45.1 us (32%)
  waiting for transfers between devices  36.2 us (26%)
  blocking collectives  32.2 us (23%)
  Pallas kernels  20.2 us (14%)
  local copies, waits for them, and re-layouts  4.66 us (3%)
  between operations  1.68 us (1%)
    ppermute x29, starting transfers between devices, move(): return lax.ppermute(array, 'shard', pairs)  45.1 us
    ppermute x29, waiting for transfers between devices, move(): return lax.ppermute(array, 'shard', pairs)  36.2 us
    pallas_call x31, Pallas kernels, call(): pl.pallas_call(body, out_shape=[jax.ShapeDtypeStruct(s, t) for s, t in ou...  20.2 us
    all_to_all x1, blocking collectives, local(): lax.all_to_all(stepped, 'worker', split_axis=1, concat_axis=0, tiled=True)  20 us
    all_to_all x1, blocking collectives, local(): lax.all_to_all(spread, 'worker', split_axis=0, concat_axis=1, tiled=True)  12.2 us
    unnamed x22, local copies, waits for them, and re-layouts  3.67 us
  transfers between devices with their start and end apart: 29, of which 15 were waited for; matrix products, arithmetic and copies ran while one was open for 0% of the time, Pallas kernels for 10%

profile of v2, /device:TPU:64, one launch (start us, length us, event | category | flops | bytes accessed | tf_op | source)
XLA Modules:
  0.0 141.1 jit_solution(9066918232734204995)
XLA Ops:
  2.0 1.8 %pick.1 = (bf16[512,512]{1,0:T(8,128)(2,1)S(1)}, bf16[512,512]{1,0:T(8,128)(2,1)S(1)}) custom-call(bf16[512,1024]{1,0:T(8,128)(2,1)S(1)} %copy-done.5), custom_call_target="tpu_custom_call" | custom-call | flops 49999998976 | bytes 500000000 | tf_op jit(solution)/shard_map/pick/pallas_call | solution.py:67
  4.3 3.2 %product.5 = (bf16[512,2048]{1,0:T(8,128)(2,1)S(1)}, bf16[512,2048]{1,0:T(8,128)(2,1)S(1)}) custom-call(bf16[512,512]{1,0:T(8,128)(2,1)S(1)} %get-tuple-element.23.refs_0_.refs_1_, bf16[512,512]{1,0:T(8,128)(2,1)S(1)} %get-tuple-element.23.refs_0_.refs_1_, bf16[512,512]{1,0:T(8,128)(2,1)S(1)} %get-tuple-element.24.refs_2_, bf16[512,8192]{1,0:T(8,128)(2,1)S(1)} %copy-done.4), custom_call_target="tpu_custom_call" | custom-call | flops 49999998976 | bytes 500000000 | tf_op jit(solution)/shard_map/product/pallas_call | solution.py:67
  7.7 3.2 %product.6 = (bf16[512,2048]{1,0:T(8,128)(2,1)S(1)}, bf16[512,2048]{1,0:T(8,128)(2,1)S(1)}) custom-call(bf16[512,2048]{1,0:T(8,128)(2,1)S(1)} %get-tuple-element.25.refs_0_.refs_1_, bf16[512,512]{1,0:T(8,128)(2,1)S(1)} %get-tuple-element.23.refs_0_.refs_1_, bf16[512,512]{1,0:T(8,128)(2,1)S(1)} %get-tuple-element.24.refs_2_, bf16[512,8192]{1,0:T(8,128)(2,1)S(1)} %copy-done.4), custom_call_target="tpu_custom_call" | custom-call | flops 49999998976 | bytes 500000000 | tf_op jit(solution)/shard_map/product/pallas_call | solution.py:67
  13.1 2.4 %product.7 = (bf16[512,1536]{1,0:T(8,128)(2,1)S(1)}, bf16[512,1536]{1,0:T(8,128)(2,1)S(1)}) custom-call(bf16[128,2048]{1,0:T(8,128)(2,1)S(1)} %relay.19.refs_0_, bf16[512,512]{1,0:T(8,128)(2,1)S(1)} %get-tuple-element.23.refs_0_.refs_1_, bf16[512,512]{1,0:T(8,128)(2,1)S(1)} %get-tuple-element.24.refs_2_, bf16[512,8192]{1,0:T(8,128)(2,1)S(1)} %copy-done.4), custom_call_target="tpu_custom_call" | custom-call | flops 49999998976 | bytes 500000000 | tf_op jit(solution)/shard_map/product/pallas_call | solution.py:67
  19.2 2.4 %product.8 = (bf16[512,1536]{1,0:T(8,128)(2,1)S(1)}, bf16[512,1536]{1,0:T(8,128)(2,1)S(1)}) custom-call(bf16[128,1536]{1,0:T(8,128)(2,1)S(1)} %relay.21.refs_0_, bf16[512,512]{1,0:T(8,128)(2,1)S(1)} %get-tuple-element.23.refs_0_.refs_1_, bf16[512,512]{1,0:T(8,128)(2,1)S(1)} %get-tuple-element.24.refs_2_, bf16[512,8192]{1,0:T(8,128)(2,1)S(1)} %copy-done.4), custom_call_target="tpu_custom_call" | custom-call | flops 49999998976 | bytes 500000000 | tf_op jit(solution)/shard_map/product/pallas_call | solution.py:67
  21.7 4.7 %collective-permute-start.5 = (bf16[128,1536]{1,0:T(8,128)(2,1)S(1)}, bf16[128,1536]{1,0:T(8,128)(2,1)S(1)}, u32[]{:S(2)}, u32[]{:S(2)}) collective-permute-start(bf16[128,1536]{1,0:T(8,128)(2,1)S(1)} %relay.21.refs_0_), channel_id=1, source_target_pairs={{0,8},{1,25},{2,10},{3,27},{4,12},{5,29},{6,14},{7,31},{8,16},{9,1... | collective-permute-start | bytes 1179656 | tf_op jit(solution)/shard_map/ppermute | solution.py:45
  32.4 1.7 %collective-permute-start.10 = (bf16[512,1024]{1,0:T(8,128)(2,1)S(1)}, bf16[512,1024]{1,0:T(8,128)(2,1)S(1)}, u32[]{:S(2)}, u32[]{:S(2)}) collective-permute-start(bf16[512,1024]{1,0:T(8,128)(2,1)S(1)} %get-tuple-element.34), channel_id=1, source_target_pairs={{0,1},{1,0},{2,3},{3,2},{4,5},{5,4},{6,7},{7,6},{8,9},{9,8},{10,11... | collective-permute-start | bytes 3145736 | tf_op jit(solution)/shard_map/ppermute | solution.py:45
  36.0 4.7 %collective-permute-start.9 = (bf16[128,1536]{1,0:T(8,128)(2,1)S(1)}, bf16[128,1536]{1,0:T(8,128)(2,1)S(1)}, u32[]{:S(2)}, u32[]{:S(2)}) collective-permute-start(bf16[128,1536]{1,0:T(8,128)(2,1)S(1)} %relay.24.refs_0_), channel_id=1, source_target_pairs={{0,8},{1,25},{2,10},{3,27},{4,12},{5,29},{6,14},{7,31},{8,16},{9,1... | collective-permute-start | bytes 1179656 | tf_op jit(solution)/shard_map/ppermute | solution.py:45
  42.4 2.5 %collective-permute-done.7.refs_3_ = bf16[128,2048]{1,0:T(8,128)(2,1)S(1)} collective-permute-done((bf16[128,2048]{1,0:T(8,128)(2,1)S(1)}, bf16[128,2048]{1,0:T(8,128)(2,1)S(1)}, u32[]{:S(2)}, u32[]{:S(2)}) %collective-permute-start.7) | collective-permute-done | bytes 524320 | tf_op jit(solution)/shard_map/ppermute | solution.py:45
  47.2 1.8 %collective-permute-done.9.refs_3_ = bf16[128,1536]{1,0:T(8,128)(2,1)S(1)} collective-permute-done((bf16[128,1536]{1,0:T(8,128)(2,1)S(1)}, bf16[128,1536]{1,0:T(8,128)(2,1)S(1)}, u32[]{:S(2)}, u32[]{:S(2)}) %collective-permute-start.9) | collective-permute-done | bytes 393248 | tf_op jit(solution)/shard_map/ppermute | solution.py:45
  49.2 4.7 %collective-permute-start.15 = (bf16[128,1536]{1,0:T(8,128)(2,1)S(1)}, bf16[128,1536]{1,0:T(8,128)(2,1)S(1)}, u32[]{:S(2)}, u32[]{:S(2)}) collective-permute-start(bf16[128,1536]{1,0:T(8,128)(2,1)S(1)} %relay.28.refs_0_), channel_id=1, source_target_pairs={{0,8},{1,25},{2,10},{3,27},{4,12},{5,29},{6,14},{7,31},{8,16},{9,1... | collective-permute-start | bytes 1179656 | tf_op jit(solution)/shard_map/ppermute | solution.py:45
  57.3 1.9 %collective-permute-start.16 = (bf16[32,4096]{1,0:T(8,128)(2,1)S(1)}, bf16[32,4096]{1,0:T(8,128)(2,1)S(1)}, u32[]{:S(2)}, u32[]{:S(2)}) collective-permute-start(bf16[32,4096]{1,0:T(8,128)(2,1)S(1)} %get-tuple-element.35.refs_0_), channel_id=1, source_target_pairs={{0,8},{1,25},{2,10},{3,27},{4,12},{5,29},{6,14},{7,31},{8,16},{9,1... | collective-permute-start | bytes 786440 | tf_op jit(solution)/shard_map/ppermute | solution.py:45
  59.2 1.9 %collective-permute-done.13.refs_3_ = bf16[128,1536]{1,0:T(8,128)(2,1)S(1)} collective-permute-done((bf16[128,1536]{1,0:T(8,128)(2,1)S(1)}, bf16[128,1536]{1,0:T(8,128)(2,1)S(1)}, u32[]{:S(2)}, u32[]{:S(2)}) %collective-permute-start.13) | collective-permute-done | bytes 393248 | tf_op jit(solution)/shard_map/ppermute | solution.py:45
  61.6 2.3 %collective-permute-done.14.refs_3_ = bf16[128,1024]{1,0:T(8,128)(2,1)S(1)} collective-permute-done((bf16[128,1024]{1,0:T(8,128)(2,1)S(1)}, bf16[128,1024]{1,0:T(8,128)(2,1)S(1)}, u32[]{:S(2)}, u32[]{:S(2)}) %collective-permute-start.14) | collective-permute-done | bytes 262176 | tf_op jit(solution)/shard_map/ppermute | solution.py:45
  64.8 3.2 %collective-permute-done.16.refs_2_ = bf16[32,4096]{1,0:T(8,128)(2,1)S(1)} collective-permute-done((bf16[32,4096]{1,0:T(8,128)(2,1)S(1)}, bf16[32,4096]{1,0:T(8,128)(2,1)S(1)}, u32[]{:S(2)}, u32[]{:S(2)}) %collective-permute-start.16) | collective-permute-done | bytes 262176 | tf_op jit(solution)/shard_map/ppermute | solution.py:45
  68.0 4.7 %collective-permute-start.20 = (bf16[32,4096]{1,0:T(8,128)(2,1)S(1)}, bf16[32,4096]{1,0:T(8,128)(2,1)S(1)}, u32[]{:S(2)}, u32[]{:S(2)}) collective-permute-start(bf16[32,4096]{1,0:T(8,128)(2,1)S(1)} %relay.32.refs_0_), channel_id=1, source_target_pairs={{0,8},{1,25},{2,10},{3,27},{4,12},{5,29},{6,14},{7,31},{8,16},{9,1... | collective-permute-start | bytes 786440 | tf_op jit(solution)/shard_map/ppermute | solution.py:45
  75.5 3.0 %collective-permute-done.18.refs_2_ = bf16[32,1536]{1,0:T(8,128)(2,1)S(1)} collective-permute-done((bf16[32,1536]{1,0:T(8,128)(2,1)S(1)}, bf16[32,1536]{1,0:T(8,128)(2,1)S(1)}, u32[]{:S(2)}, u32[]{:S(2)}) %collective-permute-start.18) | collective-permute-done | bytes 98336 | tf_op jit(solution)/shard_map/ppermute | solution.py:45
  79.3 4.7 %collective-permute-start.24 = (bf16[32,4096]{1,0:T(8,128)(2,1)S(1)}, bf16[32,4096]{1,0:T(8,128)(2,1)S(1)}, u32[]{:S(2)}, u32[]{:S(2)}) collective-permute-start(bf16[32,4096]{1,0:T(8,128)(2,1)S(1)} %relay.36.refs_0_), channel_id=1, source_target_pairs={{0,8},{1,25},{2,10},{3,27},{4,12},{5,29},{6,14},{7,31},{8,16},{9,1... | collective-permute-start | bytes 786440 | tf_op jit(solution)/shard_map/ppermute | solution.py:45
  86.6 4.0 %collective-permute-done.23.refs_2_ = bf16[32,1536]{1,0:T(8,128)(2,1)S(1)} collective-permute-done((bf16[32,1536]{1,0:T(8,128)(2,1)S(1)}, bf16[32,1536]{1,0:T(8,128)(2,1)S(1)}, u32[]{:S(2)}, u32[]{:S(2)}) %collective-permute-start.23) | collective-permute-done | bytes 98336 | tf_op jit(solution)/shard_map/ppermute | solution.py:45
  90.9 1.9 %collective-permute-start.28 = (bf16[32,2560]{1,0:T(8,128)(2,1)S(1)}, bf16[32,2560]{1,0:T(8,128)(2,1)S(1)}, u32[]{:S(2)}, u32[]{:S(2)}) collective-permute-start(bf16[32,2560]{1,0:T(8,128)(2,1)S(1)} %get-tuple-element.42), channel_id=1, source_target_pairs={{0,8},{1,25},{2,10},{3,27},{4,12},{5,29},{6,14},{7,31},{8,16},{9,1... | collective-permute-start | bytes 491528 | tf_op jit(solution)/shard_map/ppermute | solution.py:45
  93.8 2.8 %collective-permute-done.25.refs_6_ = bf16[32,1536]{1,0:T(8,128)(2,1)S(1)} collective-permute-done((bf16[32,1536]{1,0:T(8,128)(2,1)S(1)}, bf16[32,1536]{1,0:T(8,128)(2,1)S(1)}, u32[]{:S(2)}, u32[]{:S(2)}) %collective-permute-start.25) | collective-permute-done | bytes 98336 | tf_op jit(solution)/shard_map/ppermute | solution.py:45
  97.3 8.8 %collective-permute-done.26.refs_6_ = bf16[32,2560]{1,0:T(8,128)(2,1)S(1)} collective-permute-done((bf16[32,2560]{1,0:T(8,128)(2,1)S(1)}, bf16[32,2560]{1,0:T(8,128)(2,1)S(1)}, u32[]{:S(2)}, u32[]{:S(2)}) %collective-permute-start.26) | collective-permute-done | bytes 163872 | tf_op jit(solution)/shard_map/ppermute | solution.py:45
  107.2 20.0 %all_to_all.29 = f32[32,8,1024]{2,0,1:T(8,128)S(1)} all-to-all(f32[32,8,1024]{2,0,1:T(8,128)S(1)} %bitcast.20), channel_id=1, replica_groups=mesh['worker'=8,'shard'=32] {'worker'}, dimensions={1} | all-to-all | bytes 2097152 | tf_op jit(solution)/shard_map/all_to_all | solution.py:280
  128.1 12.2 %all_to_all.30 = bf16[8,32,1024]{2,1,0:T(8,128)(2,1)S(1)} all-to-all(bf16[8,32,1024]{2,1,0:T(8,128)(2,1)S(1)} %broadcast_in_dim.2), channel_id=1, replica_groups=mesh['worker'=8,'shard'=32] {'worker'}, dimensions={0} | all-to-all | bytes 1048576 | tf_op jit(solution)/shard_map/all_to_all | solution.py:286
  (96 shorter events, 34.9 us)
Async XLA Ops:
  10.9 6.5 %collective-permute-start.1 = (bf16[512,2048]{1,0:T(8,128)(2,1)S(1)}, bf16[512,2048]{1,0:T(8,128)(2,1)S(1)}, u32[]{:S(2)}, u32[]{:S(2)}) collective-permute-start(bf16[512,2048]{1,0:T(8,128)(2,1)S(1)} %get-tuple-element.29), channel_id=1, source_target_pairs={{0,1},{1,0},{2,3},{3,2},{4,5},{5,4},{6,7},{7,6},{8,9},{9,8},{10,11... | collective-permute-start | bytes 6291464 | tf_op jit(solution)/shard_map/ppermute | solution.py:45
  15.8 12.2 %collective-permute-start.3 = (bf16[128,2048]{1,0:T(8,128)(2,1)S(1)}, bf16[128,2048]{1,0:T(8,128)(2,1)S(1)}, u32[]{:S(2)}, u32[]{:S(2)}) collective-permute-start(bf16[128,2048]{1,0:T(8,128)(2,1)S(1)} %relay.19.refs_0_), channel_id=1, source_target_pairs={{0,2},{1,7},{2,4},{3,1},{4,6},{5,3},{6,0},{7,5},{8,10},{9,15},{10,... | collective-permute-start | bytes 1572872 | tf_op jit(solution)/shard_map/ppermute | solution.py:45
  17.5 14.3 %collective-permute-start.4 = (bf16[128,2048]{1,0:T(8,128)(2,1)S(1)}, bf16[128,2048]{1,0:T(8,128)(2,1)S(1)}, u32[]{:S(2)}, u32[]{:S(2)}) collective-permute-start(bf16[128,2048]{1,0:T(8,128)(2,1)S(1)} %relay.20.refs_0_), channel_id=1, source_target_pairs={{0,2},{1,7},{2,4},{3,1},{4,6},{5,3},{6,0},{7,5},{8,10},{9,15},{10,... | collective-permute-start | bytes 1572872 | tf_op jit(solution)/shard_map/ppermute | solution.py:45
  21.7 14.2 %collective-permute-start.5 = (bf16[128,1536]{1,0:T(8,128)(2,1)S(1)}, bf16[128,1536]{1,0:T(8,128)(2,1)S(1)}, u32[]{:S(2)}, u32[]{:S(2)}) collective-permute-start(bf16[128,1536]{1,0:T(8,128)(2,1)S(1)} %relay.21.refs_0_), channel_id=1, source_target_pairs={{0,8},{1,25},{2,10},{3,27},{4,12},{5,29},{6,14},{7,31},{8,16},{9,1... | collective-permute-start | bytes 1179656 | tf_op jit(solution)/shard_map/ppermute | solution.py:45
  26.4 19.1 %collective-permute-start.8 = (bf16[512,1536]{1,0:T(8,128)(2,1)S(1)}, bf16[512,1536]{1,0:T(8,128)(2,1)S(1)}, u32[]{:S(2)}, u32[]{:S(2)}) collective-permute-start(bf16[512,1536]{1,0:T(8,128)(2,1)S(1)} %get-tuple-element.33), channel_id=1, source_target_pairs={{0,1},{1,0},{2,3},{3,2},{4,5},{5,4},{6,7},{7,6},{8,9},{9,8},{10,11... | collective-permute-start | bytes 4718600 | tf_op jit(solution)/shard_map/ppermute | solution.py:45
  28.8 11.8 %collective-permute-start.6 = (bf16[128,2048]{1,0:T(8,128)(2,1)S(1)}, bf16[128,2048]{1,0:T(8,128)(2,1)S(1)}, u32[]{:S(2)}, u32[]{:S(2)}) collective-permute-start(bf16[128,2048]{1,0:T(8,128)(2,1)S(1)} %relay.22.refs_0_), channel_id=1, source_target_pairs={{0,2},{1,7},{2,4},{3,1},{4,6},{5,3},{6,0},{7,5},{8,10},{9,15},{10,... | collective-permute-start | bytes 1572872 | tf_op jit(solution)/shard_map/ppermute | solution.py:45
  32.0 12.9 %collective-permute-start.7 = (bf16[128,2048]{1,0:T(8,128)(2,1)S(1)}, bf16[128,2048]{1,0:T(8,128)(2,1)S(1)}, u32[]{:S(2)}, u32[]{:S(2)}) collective-permute-start(bf16[128,2048]{1,0:T(8,128)(2,1)S(1)} %relay.23.refs_0_), channel_id=1, source_target_pairs={{0,2},{1,7},{2,4},{3,1},{4,6},{5,3},{6,0},{7,5},{8,10},{9,15},{10,... | collective-permute-start | bytes 1572872 | tf_op jit(solution)/shard_map/ppermute | solution.py:45
  32.4 21.4 %collective-permute-start.10 = (bf16[512,1024]{1,0:T(8,128)(2,1)S(1)}, bf16[512,1024]{1,0:T(8,128)(2,1)S(1)}, u32[]{:S(2)}, u32[]{:S(2)}) collective-permute-start(bf16[512,1024]{1,0:T(8,128)(2,1)S(1)} %get-tuple-element.34), channel_id=1, source_target_pairs={{0,1},{1,0},{2,3},{3,2},{4,5},{5,4},{6,7},{7,6},{8,9},{9,8},{10,11... | collective-permute-start | bytes 3145736 | tf_op jit(solution)/shard_map/ppermute | solution.py:45
  36.0 13.1 %collective-permute-start.9 = (bf16[128,1536]{1,0:T(8,128)(2,1)S(1)}, bf16[128,1536]{1,0:T(8,128)(2,1)S(1)}, u32[]{:S(2)}, u32[]{:S(2)}) collective-permute-start(bf16[128,1536]{1,0:T(8,128)(2,1)S(1)} %relay.24.refs_0_), channel_id=1, source_target_pairs={{0,8},{1,25},{2,10},{3,27},{4,12},{5,29},{6,14},{7,31},{8,16},{9,1... | collective-permute-start | bytes 1179656 | tf_op jit(solution)/shard_map/ppermute | solution.py:45
  40.8 16.1 %collective-permute-start.11 = (bf16[128,2048]{1,0:T(8,128)(2,1)S(1)}, bf16[128,2048]{1,0:T(8,128)(2,1)S(1)}, u32[]{:S(2)}, u32[]{:S(2)}) collective-permute-start(bf16[128,2048]{1,0:T(8,128)(2,1)S(1)} %relay.25.refs_0_), channel_id=1, source_target_pairs={{0,2},{1,7},{2,4},{3,1},{4,6},{5,3},{6,0},{7,5},{8,10},{9,15},{10,... | collective-permute-start | bytes 1572872 | tf_op jit(solution)/shard_map/ppermute | solution.py:45
  45.1 11.8 %collective-permute-start.12 = (bf16[128,2048]{1,0:T(8,128)(2,1)S(1)}, bf16[128,2048]{1,0:T(8,128)(2,1)S(1)}, u32[]{:S(2)}, u32[]{:S(2)}) collective-permute-start(bf16[128,2048]{1,0:T(8,128)(2,1)S(1)} %relay.26.refs_0_), channel_id=1, source_target_pairs={{0,2},{1,7},{2,4},{3,1},{4,6},{5,3},{6,0},{7,5},{8,10},{9,15},{10,... | collective-permute-start | bytes 1572872 | tf_op jit(solution)/shard_map/ppermute | solution.py:45
  45.6 15.6 %collective-permute-start.13 = (bf16[128,1536]{1,0:T(8,128)(2,1)S(1)}, bf16[128,1536]{1,0:T(8,128)(2,1)S(1)}, u32[]{:S(2)}, u32[]{:S(2)}) collective-permute-start(bf16[128,1536]{1,0:T(8,128)(2,1)S(1)} %relay.27.refs_0_), channel_id=1, source_target_pairs={{0,2},{1,7},{2,4},{3,1},{4,6},{5,3},{6,0},{7,5},{8,10},{9,15},{10,... | collective-permute-start | bytes 1179656 | tf_op jit(solution)/shard_map/ppermute | solution.py:45
  49.2 15.4 %collective-permute-start.15 = (bf16[128,1536]{1,0:T(8,128)(2,1)S(1)}, bf16[128,1536]{1,0:T(8,128)(2,1)S(1)}, u32[]{:S(2)}, u32[]{:S(2)}) collective-permute-start(bf16[128,1536]{1,0:T(8,128)(2,1)S(1)} %relay.28.refs_0_), channel_id=1, source_target_pairs={{0,8},{1,25},{2,10},{3,27},{4,12},{5,29},{6,14},{7,31},{8,16},{9,1... | collective-permute-start | bytes 1179656 | tf_op jit(solution)/shard_map/ppermute | solution.py:45
  53.9 10.0 %collective-permute-start.14 = (bf16[128,1024]{1,0:T(8,128)(2,1)S(1)}, bf16[128,1024]{1,0:T(8,128)(2,1)S(1)}, u32[]{:S(2)}, u32[]{:S(2)}) collective-permute-start(bf16[128,1024]{1,0:T(8,128)(2,1)S(1)} %relay.29.refs_0_), channel_id=1, source_target_pairs={{0,2},{1,7},{2,4},{3,1},{4,6},{5,3},{6,0},{7,5},{8,10},{9,15},{10,... | collective-permute-start | bytes 786440 | tf_op jit(solution)/shard_map/ppermute | solution.py:45
  57.3 10.6 %collective-permute-start.16 = (bf16[32,4096]{1,0:T(8,128)(2,1)S(1)}, bf16[32,4096]{1,0:T(8,128)(2,1)S(1)}, u32[]{:S(2)}, u32[]{:S(2)}) collective-permute-start(bf16[32,4096]{1,0:T(8,128)(2,1)S(1)} %get-tuple-element.35.refs_0_), channel_id=1, source_target_pairs={{0,8},{1,25},{2,10},{3,27},{4,12},{5,29},{6,14},{7,31},{8,16},{9,1... | collective-permute-start | bytes 786440 | tf_op jit(solution)/shard_map/ppermute | solution.py:45
  61.3 12.4 %collective-permute-start.17 = (bf16[128,1536]{1,0:T(8,128)(2,1)S(1)}, bf16[128,1536]{1,0:T(8,128)(2,1)S(1)}, u32[]{:S(2)}, u32[]{:S(2)}) collective-permute-start(bf16[128,1536]{1,0:T(8,128)(2,1)S(1)} %relay.30.refs_0_), channel_id=1, source_target_pairs={{0,2},{1,7},{2,4},{3,1},{4,6},{5,3},{6,0},{7,5},{8,10},{9,15},{10,... | collective-permute-start | bytes 1179656 | tf_op jit(solution)/shard_map/ppermute | solution.py:45
  64.0 14.5 %collective-permute-start.19 = (bf16[128,1024]{1,0:T(8,128)(2,1)S(1)}, bf16[128,1024]{1,0:T(8,128)(2,1)S(1)}, u32[]{:S(2)}, u32[]{:S(2)}) collective-permute-start(bf16[128,1024]{1,0:T(8,128)(2,1)S(1)} %relay.31.refs_0_), channel_id=1, source_target_pairs={{0,2},{1,7},{2,4},{3,1},{4,6},{5,3},{6,0},{7,5},{8,10},{9,15},{10,... | collective-permute-start | bytes 786440 | tf_op jit(solution)/shard_map/ppermute | solution.py:45
  68.0 11.3 %collective-permute-start.20 = (bf16[32,4096]{1,0:T(8,128)(2,1)S(1)}, bf16[32,4096]{1,0:T(8,128)(2,1)S(1)}, u32[]{:S(2)}, u32[]{:S(2)}) collective-permute-start(bf16[32,4096]{1,0:T(8,128)(2,1)S(1)} %relay.32.refs_0_), channel_id=1, source_target_pairs={{0,8},{1,25},{2,10},{3,27},{4,12},{5,29},{6,14},{7,31},{8,16},{9,1... | collective-permute-start | bytes 786440 | tf_op jit(solution)/shard_map/ppermute | solution.py:45
  73.8 12.5 %collective-permute-start.21 = (bf16[128,1536]{1,0:T(8,128)(2,1)S(1)}, bf16[128,1536]{1,0:T(8,128)(2,1)S(1)}, u32[]{:S(2)}, u32[]{:S(2)}) collective-permute-start(bf16[128,1536]{1,0:T(8,128)(2,1)S(1)} %relay.33.refs_0_), channel_id=1, source_target_pairs={{0,2},{1,7},{2,4},{3,1},{4,6},{5,3},{6,0},{7,5},{8,10},{9,15},{10,... | collective-permute-start | bytes 1179656 | tf_op jit(solution)/shard_map/ppermute | solution.py:45
  78.7 7.7 %collective-permute-start.22 = (bf16[128,1024]{1,0:T(8,128)(2,1)S(1)}, bf16[128,1024]{1,0:T(8,128)(2,1)S(1)}, u32[]{:S(2)}, u32[]{:S(2)}) collective-permute-start(bf16[128,1024]{1,0:T(8,128)(2,1)S(1)} %relay.35.refs_0_), channel_id=1, source_target_pairs={{0,2},{1,7},{2,4},{3,1},{4,6},{5,3},{6,0},{7,5},{8,10},{9,15},{10,... | collective-permute-start | bytes 786440 | tf_op jit(solution)/shard_map/ppermute | solution.py:45
  79.3 13.4 %collective-permute-start.24 = (bf16[32,4096]{1,0:T(8,128)(2,1)S(1)}, bf16[32,4096]{1,0:T(8,128)(2,1)S(1)}, u32[]{:S(2)}, u32[]{:S(2)}) collective-permute-start(bf16[32,4096]{1,0:T(8,128)(2,1)S(1)} %relay.36.refs_0_), channel_id=1, source_target_pairs={{0,8},{1,25},{2,10},{3,27},{4,12},{5,29},{6,14},{7,31},{8,16},{9,1... | collective-permute-start | bytes 786440 | tf_op jit(solution)/shard_map/ppermute | solution.py:45
  86.6 19.5 %collective-permute-start.26 = (bf16[32,2560]{1,0:T(8,128)(2,1)S(1)}, bf16[32,2560]{1,0:T(8,128)(2,1)S(1)}, u32[]{:S(2)}, u32[]{:S(2)}) collective-permute-start(bf16[32,2560]{1,0:T(8,128)(2,1)S(1)} %get-tuple-element.39.refs_0_), channel_id=1, source_target_pairs={{0,24},{1,9},{2,26},{3,11},{4,28},{5,13},{6,30},{7,15},{8,0},{9,17... | collective-permute-start | bytes 491528 | tf_op jit(solution)/shard_map/ppermute | solution.py:45
  90.8 15.3 %collective-permute-start.27 = (bf16[32,2560]{1,0:T(8,128)(2,1)S(1)}, bf16[32,2560]{1,0:T(8,128)(2,1)S(1)}, u32[]{:S(2)}, u32[]{:S(2)}) collective-permute-start(bf16[32,2560]{1,0:T(8,128)(2,1)S(1)} %get-tuple-element.41), channel_id=1, source_target_pairs={{0,16},{1,17},{2,18},{3,19},{4,20},{5,21},{6,22},{7,23},{8,24},{9,... | collective-permute-start | bytes 491528 | tf_op jit(solution)/shard_map/ppermute | solution.py:45
  90.9 15.2 %collective-permute-start.28 = (bf16[32,2560]{1,0:T(8,128)(2,1)S(1)}, bf16[32,2560]{1,0:T(8,128)(2,1)S(1)}, u32[]{:S(2)}, u32[]{:S(2)}) collective-permute-start(bf16[32,2560]{1,0:T(8,128)(2,1)S(1)} %get-tuple-element.42), channel_id=1, source_target_pairs={{0,8},{1,25},{2,10},{3,27},{4,12},{5,29},{6,14},{7,31},{8,16},{9,1... | collective-permute-start | bytes 491528 | tf_op jit(solution)/shard_map/ppermute | solution.py:45
  (16 other events, 101.2 us)

commit v3 on v2

--- a/solution.py
+++ b/solution.py
@@ -265,12 +265,12 @@
     run("relay", relay("d", "y"))
     run("settle", settle("e", "y"))
     run("relay", relay("ab", "z"))
+    run("relay", relay("e", "y"), cost=LATE_COST)
     run("relay", relay("c", "y"), cost=LATE_COST)
-    run("relay", relay("e", "y"), cost=LATE_COST)
     run("relay", relay("d", "y"), cost=LATE_COST)
     run("relay", relay("ab", "z"), cost=LATE_COST)
-    run("settle", settle("cd", "z", direct=True), cost=LATE_COST)
-    run("relay", relay("e", "y"), cost=LATE_COST)
+    run("relay", relay("e", "y"))
+    run("settle", settle("cd", "z", direct=True))
     run("adam", adam("ab"), scalars=(fix,))
     run("adam", adam("e"), scalars=(fix,))
     run("adam", adam("cd"), scalars=(fix,))

time: 141 us -> 140 us (level)
  waiting for transfers between devices: 36.2 us -> 28.6 us
  starting transfers between devices: 45.1 us -> 52.4 us
  local copies, waits for them, and re-layouts: 4.66 us -> 2.87 us
    ppermute x29, waiting for transfers between devices: 36.2 us -> 28.6 us  [move(): return lax.ppermute(array, 'shard', pairs)]
    ppermute x29, starting transfers between devices: 45.1 us -> 52.4 us  [move(): return lax.ppermute(array, 'shard', pairs)]
    unnamed x22 -> x18, local copies, waits for them, and re-layouts: 3.67 us -> 1.88 us
  transfers between devices with their start and end apart: 29 -> 29, of which waited for: 15 -> 13; matrix products, arithmetic and copies ran while one was open for 0% -> 0% of each run, Pallas kernels for 10% -> 10%
where the time goes in v3:
time: 140 us; the launch traced here: 139 us
  starting transfers between devices  52.4 us (37%)
  blocking collectives  32.4 us (23%)
  waiting for transfers between devices  28.6 us (20%)
  Pallas kernels  20.2 us (14%)
  local copies, waits for them, and re-layouts  2.87 us (2%)
  between operations  1.68 us (1%)
    ppermute x29, starting transfers between devices, move(): return lax.ppermute(array, 'shard', pairs)  52.4 us
    ppermute x29, waiting for transfers between devices, move(): return lax.ppermute(array, 'shard', pairs)  28.6 us
    pallas_call x31, Pallas kernels, call(): pl.pallas_call(body, out_shape=[jax.ShapeDtypeStruct(s, t) for s, t in ou...  20.2 us
    all_to_all x1, blocking collectives, local(): lax.all_to_all(stepped, 'worker', split_axis=1, concat_axis=0, tiled=True)  20.2 us
    all_to_all x1, blocking collectives, local(): lax.all_to_all(spread, 'worker', split_axis=0, concat_axis=1, tiled=True)  12.2 us
  transfers between devices with their start and end apart: 29, of which 13 were waited for; matrix products, arithmetic and copies ran while one was open for 0% of the time, Pallas kernels for 10%

profile of v3, /device:TPU:64, one launch (start us, length us, event | category | flops | bytes accessed | tf_op | source)
XLA Modules:
  0.0 139.1 jit_solution(5853770219633007)
XLA Ops:
  2.0 1.8 %pick.1 = (bf16[512,512]{1,0:T(8,128)(2,1)S(1)}, bf16[512,512]{1,0:T(8,128)(2,1)S(1)}) custom-call(bf16[512,1024]{1,0:T(8,128)(2,1)S(1)} %copy-done.3), custom_call_target="tpu_custom_call" | custom-call | flops 49999998976 | bytes 500000000 | tf_op jit(solution)/shard_map/pick/pallas_call | solution.py:67
  4.3 3.2 %product.5 = (bf16[512,2048]{1,0:T(8,128)(2,1)S(1)}, bf16[512,2048]{1,0:T(8,128)(2,1)S(1)}) custom-call(bf16[512,512]{1,0:T(8,128)(2,1)S(1)} %get-tuple-element.23.refs_0_.refs_1_, bf16[512,512]{1,0:T(8,128)(2,1)S(1)} %get-tuple-element.23.refs_0_.refs_1_, bf16[512,512]{1,0:T(8,128)(2,1)S(1)} %get-tuple-element.24.refs_2_, bf16[512,8192]{1,0:T(8,128)(2,1)S(1)} %copy-done.2), custom_call_target="tpu_custom_call" | custom-call | flops 49999998976 | bytes 500000000 | tf_op jit(solution)/shard_map/product/pallas_call | solution.py:67
  7.7 3.2 %product.6 = (bf16[512,2048]{1,0:T(8,128)(2,1)S(1)}, bf16[512,2048]{1,0:T(8,128)(2,1)S(1)}) custom-call(bf16[512,2048]{1,0:T(8,128)(2,1)S(1)} %get-tuple-element.25.refs_0_.refs_1_, bf16[512,512]{1,0:T(8,128)(2,1)S(1)} %get-tuple-element.23.refs_0_.refs_1_, bf16[512,512]{1,0:T(8,128)(2,1)S(1)} %get-tuple-element.24.refs_2_, bf16[512,8192]{1,0:T(8,128)(2,1)S(1)} %copy-done.2), custom_call_target="tpu_custom_call" | custom-call | flops 49999998976 | bytes 500000000 | tf_op jit(solution)/shard_map/product/pallas_call | solution.py:67
  11.9 2.4 %product.7 = (bf16[512,1536]{1,0:T(8,128)(2,1)S(1)}, bf16[512,1536]{1,0:T(8,128)(2,1)S(1)}) custom-call(bf16[128,2048]{1,0:T(8,128)(2,1)S(1)} %relay.19.refs_0_, bf16[512,512]{1,0:T(8,128)(2,1)S(1)} %get-tuple-element.23.refs_0_.refs_1_, bf16[512,512]{1,0:T(8,128)(2,1)S(1)} %get-tuple-element.24.refs_2_, bf16[512,8192]{1,0:T(8,128)(2,1)S(1)} %copy-done.2), custom_call_target="tpu_custom_call" | custom-call | flops 49999998976 | bytes 500000000 | tf_op jit(solution)/shard_map/product/pallas_call | solution.py:67
  16.3 1.7 %collective-permute-start.4 = (bf16[128,2048]{1,0:T(8,128)(2,1)S(1)}, bf16[128,2048]{1,0:T(8,128)(2,1)S(1)}, u32[]{:S(2)}, u32[]{:S(2)}) collective-permute-start(bf16[128,2048]{1,0:T(8,128)(2,1)S(1)} %relay.20.refs_0_), channel_id=1, source_target_pairs={{0,2},{1,7},{2,4},{3,1},{4,6},{5,3},{6,0},{7,5},{8,10},{9,15},{10,... | collective-permute-start | bytes 1572872 | tf_op jit(solution)/shard_map/ppermute | solution.py:45
  18.0 2.4 %product.8 = (bf16[512,1536]{1,0:T(8,128)(2,1)S(1)}, bf16[512,1536]{1,0:T(8,128)(2,1)S(1)}) custom-call(bf16[128,1536]{1,0:T(8,128)(2,1)S(1)} %relay.21.refs_0_, bf16[512,512]{1,0:T(8,128)(2,1)S(1)} %get-tuple-element.23.refs_0_.refs_1_, bf16[512,512]{1,0:T(8,128)(2,1)S(1)} %get-tuple-element.24.refs_2_, bf16[512,8192]{1,0:T(8,128)(2,1)S(1)} %copy-done.2), custom_call_target="tpu_custom_call" | custom-call | flops 49999998976 | bytes 500000000 | tf_op jit(solution)/shard_map/product/pallas_call | solution.py:67
  20.4 4.7 %collective-permute-start.5 = (bf16[128,1536]{1,0:T(8,128)(2,1)S(1)}, bf16[128,1536]{1,0:T(8,128)(2,1)S(1)}, u32[]{:S(2)}, u32[]{:S(2)}) collective-permute-start(bf16[128,1536]{1,0:T(8,128)(2,1)S(1)} %relay.21.refs_0_), channel_id=1, source_target_pairs={{0,8},{1,25},{2,10},{3,27},{4,12},{5,29},{6,14},{7,31},{8,16},{9,1... | collective-permute-start | bytes 1179656 | tf_op jit(solution)/shard_map/ppermute | solution.py:45
  28.6 2.0 %collective-permute-done.4.refs_3_ = bf16[128,2048]{1,0:T(8,128)(2,1)S(1)} collective-permute-done((bf16[128,2048]{1,0:T(8,128)(2,1)S(1)}, bf16[128,2048]{1,0:T(8,128)(2,1)S(1)}, u32[]{:S(2)}, u32[]{:S(2)}) %collective-permute-start.4) | collective-permute-done | bytes 524320 | tf_op jit(solution)/shard_map/ppermute | solution.py:45
  31.2 1.7 %collective-permute-start.10 = (bf16[512,1024]{1,0:T(8,128)(2,1)S(1)}, bf16[512,1024]{1,0:T(8,128)(2,1)S(1)}, u32[]{:S(2)}, u32[]{:S(2)}) collective-permute-start(bf16[512,1024]{1,0:T(8,128)(2,1)S(1)} %get-tuple-element.34), channel_id=1, source_target_pairs={{0,1},{1,0},{2,3},{3,2},{4,5},{5,4},{6,7},{7,6},{8,9},{9,8},{10,11... | collective-permute-start | bytes 3145736 | tf_op jit(solution)/shard_map/ppermute | solution.py:45
  34.7 4.7 %collective-permute-start.9 = (bf16[128,1536]{1,0:T(8,128)(2,1)S(1)}, bf16[128,1536]{1,0:T(8,128)(2,1)S(1)}, u32[]{:S(2)}, u32[]{:S(2)}) collective-permute-start(bf16[128,1536]{1,0:T(8,128)(2,1)S(1)} %relay.24.refs_0_), channel_id=1, source_target_pairs={{0,8},{1,25},{2,10},{3,27},{4,12},{5,29},{6,14},{7,31},{8,16},{9,1... | collective-permute-start | bytes 1179656 | tf_op jit(solution)/shard_map/ppermute | solution.py:45
  41.2 1.9 %collective-permute-done.7.refs_3_ = bf16[128,2048]{1,0:T(8,128)(2,1)S(1)} collective-permute-done((bf16[128,2048]{1,0:T(8,128)(2,1)S(1)}, bf16[128,2048]{1,0:T(8,128)(2,1)S(1)}, u32[]{:S(2)}, u32[]{:S(2)}) %collective-permute-start.7) | collective-permute-done | bytes 524320 | tf_op jit(solution)/shard_map/ppermute | solution.py:45
  45.4 2.4 %collective-permute-done.9.refs_3_ = bf16[128,1536]{1,0:T(8,128)(2,1)S(1)} collective-permute-done((bf16[128,1536]{1,0:T(8,128)(2,1)S(1)}, bf16[128,1536]{1,0:T(8,128)(2,1)S(1)}, u32[]{:S(2)}, u32[]{:S(2)}) %collective-permute-start.9) | collective-permute-done | bytes 393248 | tf_op jit(solution)/shard_map/ppermute | solution.py:45
  48.0 4.7 %collective-permute-start.15 = (bf16[128,1536]{1,0:T(8,128)(2,1)S(1)}, bf16[128,1536]{1,0:T(8,128)(2,1)S(1)}, u32[]{:S(2)}, u32[]{:S(2)}) collective-permute-start(bf16[128,1536]{1,0:T(8,128)(2,1)S(1)} %relay.28.refs_0_), channel_id=1, source_target_pairs={{0,8},{1,25},{2,10},{3,27},{4,12},{5,29},{6,14},{7,31},{8,16},{9,1... | collective-permute-start | bytes 1179656 | tf_op jit(solution)/shard_map/ppermute | solution.py:45
  56.1 1.9 %collective-permute-start.16 = (bf16[32,4096]{1,0:T(8,128)(2,1)S(1)}, bf16[32,4096]{1,0:T(8,128)(2,1)S(1)}, u32[]{:S(2)}, u32[]{:S(2)}) collective-permute-start(bf16[32,4096]{1,0:T(8,128)(2,1)S(1)} %get-tuple-element.35.refs_0_), channel_id=1, source_target_pairs={{0,8},{1,25},{2,10},{3,27},{4,12},{5,29},{6,14},{7,31},{8,16},{9,1... | collective-permute-start | bytes 786440 | tf_op jit(solution)/shard_map/ppermute | solution.py:45
  58.0 1.9 %collective-permute-done.13.refs_3_ = bf16[128,1536]{1,0:T(8,128)(2,1)S(1)} collective-permute-done((bf16[128,1536]{1,0:T(8,128)(2,1)S(1)}, bf16[128,1536]{1,0:T(8,128)(2,1)S(1)}, u32[]{:S(2)}, u32[]{:S(2)}) %collective-permute-start.13) | collective-permute-done | bytes 393248 | tf_op jit(solution)/shard_map/ppermute | solution.py:45
  60.4 2.3 %collective-permute-done.14.refs_3_ = bf16[128,1024]{1,0:T(8,128)(2,1)S(1)} collective-permute-done((bf16[128,1024]{1,0:T(8,128)(2,1)S(1)}, bf16[128,1024]{1,0:T(8,128)(2,1)S(1)}, u32[]{:S(2)}, u32[]{:S(2)}) %collective-permute-start.14) | collective-permute-done | bytes 262176 | tf_op jit(solution)/shard_map/ppermute | solution.py:45
  66.8 4.7 %collective-permute-start.20 = (bf16[32,4096]{1,0:T(8,128)(2,1)S(1)}, bf16[32,4096]{1,0:T(8,128)(2,1)S(1)}, u32[]{:S(2)}, u32[]{:S(2)}) collective-permute-start(bf16[32,4096]{1,0:T(8,128)(2,1)S(1)} %relay.32.refs_0_), channel_id=1, source_target_pairs={{0,8},{1,25},{2,10},{3,27},{4,12},{5,29},{6,14},{7,31},{8,16},{9,1... | collective-permute-start | bytes 786440 | tf_op jit(solution)/shard_map/ppermute | solution.py:45
  78.3 4.7 %collective-permute-start.24 = (bf16[32,4096]{1,0:T(8,128)(2,1)S(1)}, bf16[32,4096]{1,0:T(8,128)(2,1)S(1)}, u32[]{:S(2)}, u32[]{:S(2)}) collective-permute-start(bf16[32,4096]{1,0:T(8,128)(2,1)S(1)} %relay.36.refs_0_), channel_id=1, source_target_pairs={{0,8},{1,25},{2,10},{3,27},{4,12},{5,29},{6,14},{7,31},{8,16},{9,1... | collective-permute-start | bytes 786440 | tf_op jit(solution)/shard_map/ppermute | solution.py:45
  84.0 2.0 %collective-permute-done.23.refs_6_ = bf16[128,1024]{1,0:T(8,128)(2,1)S(1)} collective-permute-done((bf16[128,1024]{1,0:T(8,128)(2,1)S(1)}, bf16[128,1024]{1,0:T(8,128)(2,1)S(1)}, u32[]{:S(2)}, u32[]{:S(2)}) %collective-permute-start.23) | collective-permute-done | bytes 262176 | tf_op jit(solution)/shard_map/ppermute | solution.py:45
  86.7 3.7 %collective-permute-start.27 = (bf16[32,2560]{1,0:T(8,128)(2,1)S(1)}, bf16[32,2560]{1,0:T(8,128)(2,1)S(1)}, u32[]{:S(2)}, u32[]{:S(2)}) collective-permute-start(bf16[32,2560]{1,0:T(8,128)(2,1)S(1)} %get-tuple-element.41), channel_id=1, source_target_pairs={{0,16},{1,17},{2,18},{3,19},{4,20},{5,21},{6,22},{7,23},{8,24},{9,... | collective-permute-start | bytes 491528 | tf_op jit(solution)/shard_map/ppermute | solution.py:45
  90.5 2.7 %collective-permute-start.28 = (bf16[32,2560]{1,0:T(8,128)(2,1)S(1)}, bf16[32,2560]{1,0:T(8,128)(2,1)S(1)}, u32[]{:S(2)}, u32[]{:S(2)}) collective-permute-start(bf16[32,2560]{1,0:T(8,128)(2,1)S(1)} %get-tuple-element.42), channel_id=1, source_target_pairs={{0,8},{1,25},{2,10},{3,27},{4,12},{5,29},{6,14},{7,31},{8,16},{9,1... | collective-permute-start | bytes 491528 | tf_op jit(solution)/shard_map/ppermute | solution.py:45
  94.9 9.0 %collective-permute-done.26.refs_6_ = bf16[32,2560]{1,0:T(8,128)(2,1)S(1)} collective-permute-done((bf16[32,2560]{1,0:T(8,128)(2,1)S(1)}, bf16[32,2560]{1,0:T(8,128)(2,1)S(1)}, u32[]{:S(2)}, u32[]{:S(2)}) %collective-permute-start.26) | collective-permute-done | bytes 163872 | tf_op jit(solution)/shard_map/ppermute | solution.py:45
  105.0 20.2 %all_to_all.29 = f32[32,8,1024]{2,0,1:T(8,128)S(1)} all-to-all(f32[32,8,1024]{2,0,1:T(8,128)S(1)} %bitcast.20), channel_id=1, replica_groups=mesh['worker'=8,'shard'=32] {'worker'}, dimensions={1} | all-to-all | bytes 2097152 | tf_op jit(solution)/shard_map/all_to_all | solution.py:280
  126.1 12.2 %all_to_all.30 = bf16[8,32,1024]{2,1,0:T(8,128)(2,1)S(1)} all-to-all(bf16[8,32,1024]{2,1,0:T(8,128)(2,1)S(1)} %broadcast_in_dim.2), channel_id=1, replica_groups=mesh['worker'=8,'shard'=32] {'worker'}, dimensions={0} | all-to-all | bytes 1048576 | tf_op jit(solution)/shard_map/all_to_all | solution.py:286
  (92 shorter events, 35.2 us)
Async XLA Ops:
  14.6 12.2 %collective-permute-start.3 = (bf16[128,2048]{1,0:T(8,128)(2,1)S(1)}, bf16[128,2048]{1,0:T(8,128)(2,1)S(1)}, u32[]{:S(2)}, u32[]{:S(2)}) collective-permute-start(bf16[128,2048]{1,0:T(8,128)(2,1)S(1)} %relay.19.refs_0_), channel_id=1, source_target_pairs={{0,2},{1,7},{2,4},{3,1},{4,6},{5,3},{6,0},{7,5},{8,10},{9,15},{10,... | collective-permute-start | bytes 1572872 | tf_op jit(solution)/shard_map/ppermute | solution.py:45
  16.3 14.3 %collective-permute-start.4 = (bf16[128,2048]{1,0:T(8,128)(2,1)S(1)}, bf16[128,2048]{1,0:T(8,128)(2,1)S(1)}, u32[]{:S(2)}, u32[]{:S(2)}) collective-permute-start(bf16[128,2048]{1,0:T(8,128)(2,1)S(1)} %relay.20.refs_0_), channel_id=1, source_target_pairs={{0,2},{1,7},{2,4},{3,1},{4,6},{5,3},{6,0},{7,5},{8,10},{9,15},{10,... | collective-permute-start | bytes 1572872 | tf_op jit(solution)/shard_map/ppermute | solution.py:45
  20.4 14.2 %collective-permute-start.5 = (bf16[128,1536]{1,0:T(8,128)(2,1)S(1)}, bf16[128,1536]{1,0:T(8,128)(2,1)S(1)}, u32[]{:S(2)}, u32[]{:S(2)}) collective-permute-start(bf16[128,1536]{1,0:T(8,128)(2,1)S(1)} %relay.21.refs_0_), channel_id=1, source_target_pairs={{0,8},{1,25},{2,10},{3,27},{4,12},{5,29},{6,14},{7,31},{8,16},{9,1... | collective-permute-start | bytes 1179656 | tf_op jit(solution)/shard_map/ppermute | solution.py:45
  25.2 18.5 %collective-permute-start.8 = (bf16[512,1536]{1,0:T(8,128)(2,1)S(1)}, bf16[512,1536]{1,0:T(8,128)(2,1)S(1)}, u32[]{:S(2)}, u32[]{:S(2)}) collective-permute-start(bf16[512,1536]{1,0:T(8,128)(2,1)S(1)} %get-tuple-element.33), channel_id=1, source_target_pairs={{0,1},{1,0},{2,3},{3,2},{4,5},{5,4},{6,7},{7,6},{8,9},{9,8},{10,11... | collective-permute-start | bytes 4718600 | tf_op jit(solution)/shard_map/ppermute | solution.py:45
  27.0 12.4 %collective-permute-start.6 = (bf16[128,2048]{1,0:T(8,128)(2,1)S(1)}, bf16[128,2048]{1,0:T(8,128)(2,1)S(1)}, u32[]{:S(2)}, u32[]{:S(2)}) collective-permute-start(bf16[128,2048]{1,0:T(8,128)(2,1)S(1)} %relay.22.refs_0_), channel_id=1, source_target_pairs={{0,2},{1,7},{2,4},{3,1},{4,6},{5,3},{6,0},{7,5},{8,10},{9,15},{10,... | collective-permute-start | bytes 1572872 | tf_op jit(solution)/shard_map/ppermute | solution.py:45
  30.8 12.3 %collective-permute-start.7 = (bf16[128,2048]{1,0:T(8,128)(2,1)S(1)}, bf16[128,2048]{1,0:T(8,128)(2,1)S(1)}, u32[]{:S(2)}, u32[]{:S(2)}) collective-permute-start(bf16[128,2048]{1,0:T(8,128)(2,1)S(1)} %relay.23.refs_0_), channel_id=1, source_target_pairs={{0,2},{1,7},{2,4},{3,1},{4,6},{5,3},{6,0},{7,5},{8,10},{9,15},{10,... | collective-permute-start | bytes 1572872 | tf_op jit(solution)/shard_map/ppermute | solution.py:45
  31.2 21.4 %collective-permute-start.10 = (bf16[512,1024]{1,0:T(8,128)(2,1)S(1)}, bf16[512,1024]{1,0:T(8,128)(2,1)S(1)}, u32[]{:S(2)}, u32[]{:S(2)}) collective-permute-start(bf16[512,1024]{1,0:T(8,128)(2,1)S(1)} %get-tuple-element.34), channel_id=1, source_target_pairs={{0,1},{1,0},{2,3},{3,2},{4,5},{5,4},{6,7},{7,6},{8,9},{9,8},{10,11... | collective-permute-start | bytes 3145736 | tf_op jit(solution)/shard_map/ppermute | solution.py:45
  34.7 13.1 %collective-permute-start.9 = (bf16[128,1536]{1,0:T(8,128)(2,1)S(1)}, bf16[128,1536]{1,0:T(8,128)(2,1)S(1)}, u32[]{:S(2)}, u32[]{:S(2)}) collective-permute-start(bf16[128,1536]{1,0:T(8,128)(2,1)S(1)} %relay.24.refs_0_), channel_id=1, source_target_pairs={{0,8},{1,25},{2,10},{3,27},{4,12},{5,29},{6,14},{7,31},{8,16},{9,1... | collective-permute-start | bytes 1179656 | tf_op jit(solution)/shard_map/ppermute | solution.py:45
  39.6 16.1 %collective-permute-start.11 = (bf16[128,2048]{1,0:T(8,128)(2,1)S(1)}, bf16[128,2048]{1,0:T(8,128)(2,1)S(1)}, u32[]{:S(2)}, u32[]{:S(2)}) collective-permute-start(bf16[128,2048]{1,0:T(8,128)(2,1)S(1)} %relay.25.refs_0_), channel_id=1, source_target_pairs={{0,2},{1,7},{2,4},{3,1},{4,6},{5,3},{6,0},{7,5},{8,10},{9,15},{10,... | collective-permute-start | bytes 1572872 | tf_op jit(solution)/shard_map/ppermute | solution.py:45
  43.3 12.4 %collective-permute-start.12 = (bf16[128,2048]{1,0:T(8,128)(2,1)S(1)}, bf16[128,2048]{1,0:T(8,128)(2,1)S(1)}, u32[]{:S(2)}, u32[]{:S(2)}) collective-permute-start(bf16[128,2048]{1,0:T(8,128)(2,1)S(1)} %relay.26.refs_0_), channel_id=1, source_target_pairs={{0,2},{1,7},{2,4},{3,1},{4,6},{5,3},{6,0},{7,5},{8,10},{9,15},{10,... | collective-permute-start | bytes 1572872 | tf_op jit(solution)/shard_map/ppermute | solution.py:45
  43.8 16.1 %collective-permute-start.13 = (bf16[128,1536]{1,0:T(8,128)(2,1)S(1)}, bf16[128,1536]{1,0:T(8,128)(2,1)S(1)}, u32[]{:S(2)}, u32[]{:S(2)}) collective-permute-start(bf16[128,1536]{1,0:T(8,128)(2,1)S(1)} %relay.27.refs_0_), channel_id=1, source_target_pairs={{0,2},{1,7},{2,4},{3,1},{4,6},{5,3},{6,0},{7,5},{8,10},{9,15},{10,... | collective-permute-start | bytes 1179656 | tf_op jit(solution)/shard_map/ppermute | solution.py:45
  48.0 15.4 %collective-permute-start.15 = (bf16[128,1536]{1,0:T(8,128)(2,1)S(1)}, bf16[128,1536]{1,0:T(8,128)(2,1)S(1)}, u32[]{:S(2)}, u32[]{:S(2)}) collective-permute-start(bf16[128,1536]{1,0:T(8,128)(2,1)S(1)} %relay.28.refs_0_), channel_id=1, source_target_pairs={{0,8},{1,25},{2,10},{3,27},{4,12},{5,29},{6,14},{7,31},{8,16},{9,1... | collective-permute-start | bytes 1179656 | tf_op jit(solution)/shard_map/ppermute | solution.py:45
  52.7 10.0 %collective-permute-start.14 = (bf16[128,1024]{1,0:T(8,128)(2,1)S(1)}, bf16[128,1024]{1,0:T(8,128)(2,1)S(1)}, u32[]{:S(2)}, u32[]{:S(2)}) collective-permute-start(bf16[128,1024]{1,0:T(8,128)(2,1)S(1)} %relay.29.refs_0_), channel_id=1, source_target_pairs={{0,2},{1,7},{2,4},{3,1},{4,6},{5,3},{6,0},{7,5},{8,10},{9,15},{10,... | collective-permute-start | bytes 786440 | tf_op jit(solution)/shard_map/ppermute | solution.py:45
  56.1 10.7 %collective-permute-start.16 = (bf16[32,4096]{1,0:T(8,128)(2,1)S(1)}, bf16[32,4096]{1,0:T(8,128)(2,1)S(1)}, u32[]{:S(2)}, u32[]{:S(2)}) collective-permute-start(bf16[32,4096]{1,0:T(8,128)(2,1)S(1)} %get-tuple-element.35.refs_0_), channel_id=1, source_target_pairs={{0,8},{1,25},{2,10},{3,27},{4,12},{5,29},{6,14},{7,31},{8,16},{9,1... | collective-permute-start | bytes 786440 | tf_op jit(solution)/shard_map/ppermute | solution.py:45
  60.1 13.4 %collective-permute-start.18 = (bf16[128,1536]{1,0:T(8,128)(2,1)S(1)}, bf16[128,1536]{1,0:T(8,128)(2,1)S(1)}, u32[]{:S(2)}, u32[]{:S(2)}) collective-permute-start(bf16[128,1536]{1,0:T(8,128)(2,1)S(1)} %relay.30.refs_0_), channel_id=1, source_target_pairs={{0,2},{1,7},{2,4},{3,1},{4,6},{5,3},{6,0},{7,5},{8,10},{9,15},{10,... | collective-permute-start | bytes 1179656 | tf_op jit(solution)/shard_map/ppermute | solution.py:45
  62.8 12.4 %collective-permute-start.19 = (bf16[128,1024]{1,0:T(8,128)(2,1)S(1)}, bf16[128,1024]{1,0:T(8,128)(2,1)S(1)}, u32[]{:S(2)}, u32[]{:S(2)}) collective-permute-start(bf16[128,1024]{1,0:T(8,128)(2,1)S(1)} %relay.31.refs_0_), channel_id=1, source_target_pairs={{0,2},{1,7},{2,4},{3,1},{4,6},{5,3},{6,0},{7,5},{8,10},{9,15},{10,... | collective-permute-start | bytes 786440 | tf_op jit(solution)/shard_map/ppermute | solution.py:45
  66.8 11.4 %collective-permute-start.20 = (bf16[32,4096]{1,0:T(8,128)(2,1)S(1)}, bf16[32,4096]{1,0:T(8,128)(2,1)S(1)}, u32[]{:S(2)}, u32[]{:S(2)}) collective-permute-start(bf16[32,4096]{1,0:T(8,128)(2,1)S(1)} %relay.32.refs_0_), channel_id=1, source_target_pairs={{0,8},{1,25},{2,10},{3,27},{4,12},{5,29},{6,14},{7,31},{8,16},{9,1... | collective-permute-start | bytes 786440 | tf_op jit(solution)/shard_map/ppermute | solution.py:45
  73.6 12.3 %collective-permute-start.22 = (bf16[128,1536]{1,0:T(8,128)(2,1)S(1)}, bf16[128,1536]{1,0:T(8,128)(2,1)S(1)}, u32[]{:S(2)}, u32[]{:S(2)}) collective-permute-start(bf16[128,1536]{1,0:T(8,128)(2,1)S(1)} %relay.34.refs_0_), channel_id=1, source_target_pairs={{0,2},{1,7},{2,4},{3,1},{4,6},{5,3},{6,0},{7,5},{8,10},{9,15},{10,... | collective-permute-start | bytes 1179656 | tf_op jit(solution)/shard_map/ppermute | solution.py:45
  75.4 10.6 %collective-permute-start.23 = (bf16[128,1024]{1,0:T(8,128)(2,1)S(1)}, bf16[128,1024]{1,0:T(8,128)(2,1)S(1)}, u32[]{:S(2)}, u32[]{:S(2)}) collective-permute-start(bf16[128,1024]{1,0:T(8,128)(2,1)S(1)} %relay.35.refs_0_), channel_id=1, source_target_pairs={{0,2},{1,7},{2,4},{3,1},{4,6},{5,3},{6,0},{7,5},{8,10},{9,15},{10,... | collective-permute-start | bytes 786440 | tf_op jit(solution)/shard_map/ppermute | solution.py:45
  78.3 14.9 %collective-permute-start.24 = (bf16[32,4096]{1,0:T(8,128)(2,1)S(1)}, bf16[32,4096]{1,0:T(8,128)(2,1)S(1)}, u32[]{:S(2)}, u32[]{:S(2)}) collective-permute-start(bf16[32,4096]{1,0:T(8,128)(2,1)S(1)} %relay.36.refs_0_), channel_id=1, source_target_pairs={{0,8},{1,25},{2,10},{3,27},{4,12},{5,29},{6,14},{7,31},{8,16},{9,1... | collective-permute-start | bytes 786440 | tf_op jit(solution)/shard_map/ppermute | solution.py:45
  83.0 11.1 %collective-permute-start.25 = (bf16[32,1536]{1,0:T(8,128)(2,1)S(1)}, bf16[32,1536]{1,0:T(8,128)(2,1)S(1)}, u32[]{:S(2)}, u32[]{:S(2)}) collective-permute-start(bf16[32,1536]{1,0:T(8,128)(2,1)S(1)} %relay.37.refs_0_), channel_id=1, source_target_pairs={{0,2},{1,7},{2,4},{3,1},{4,6},{5,3},{6,0},{7,5},{8,10},{9,15},{10,... | collective-permute-start | bytes 294920 | tf_op jit(solution)/shard_map/ppermute | solution.py:45
  86.2 17.7 %collective-permute-start.26 = (bf16[32,2560]{1,0:T(8,128)(2,1)S(1)}, bf16[32,2560]{1,0:T(8,128)(2,1)S(1)}, u32[]{:S(2)}, u32[]{:S(2)}) collective-permute-start(bf16[32,2560]{1,0:T(8,128)(2,1)S(1)} %get-tuple-element.39.refs_0_), channel_id=1, source_target_pairs={{0,24},{1,9},{2,26},{3,11},{4,28},{5,13},{6,30},{7,15},{8,0},{9,17... | collective-permute-start | bytes 491528 | tf_op jit(solution)/shard_map/ppermute | solution.py:45
  86.7 17.2 %collective-permute-start.27 = (bf16[32,2560]{1,0:T(8,128)(2,1)S(1)}, bf16[32,2560]{1,0:T(8,128)(2,1)S(1)}, u32[]{:S(2)}, u32[]{:S(2)}) collective-permute-start(bf16[32,2560]{1,0:T(8,128)(2,1)S(1)} %get-tuple-element.41), channel_id=1, source_target_pairs={{0,16},{1,17},{2,18},{3,19},{4,20},{5,21},{6,22},{7,23},{8,24},{9,... | collective-permute-start | bytes 491528 | tf_op jit(solution)/shard_map/ppermute | solution.py:45
  90.5 13.5 %collective-permute-start.28 = (bf16[32,2560]{1,0:T(8,128)(2,1)S(1)}, bf16[32,2560]{1,0:T(8,128)(2,1)S(1)}, u32[]{:S(2)}, u32[]{:S(2)}) collective-permute-start(bf16[32,2560]{1,0:T(8,128)(2,1)S(1)} %get-tuple-element.42), channel_id=1, source_target_pairs={{0,8},{1,25},{2,10},{3,27},{4,12},{5,29},{6,14},{7,31},{8,16},{9,1... | collective-permute-start | bytes 491528 | tf_op jit(solution)/shard_map/ppermute | solution.py:45
  (14 other events, 114.4 us)

commit v4 on v3

--- a/solution.py
+++ b/solution.py
@@ -265,9 +265,9 @@
     run("relay", relay("d", "y"))
     run("settle", settle("e", "y"))
     run("relay", relay("ab", "z"))
+    run("relay", relay("c", "y"), cost=LATE_COST)
     run("relay", relay("e", "y"), cost=LATE_COST)
-    run("relay", relay("c", "y"), cost=LATE_COST)
-    run("relay", relay("d", "y"), cost=LATE_COST)
+    run("relay", relay("d", "y"))
     run("relay", relay("ab", "z"), cost=LATE_COST)
     run("relay", relay("e", "y"))
     run("settle", settle("cd", "z", direct=True))

time: 140 us -> 137 us (0.979)
  starting transfers between devices: 52.4 us -> 49.9 us
    ppermute x29, starting transfers between devices: 52.4 us -> 49.9 us  [move(): return lax.ppermute(array, 'shard', pairs)]
  transfers between devices with their start and end apart: 29 -> 29, of which waited for: 13 -> 14; matrix products, arithmetic and copies ran while one was open for 0% -> 0% of each run, Pallas kernels for 10% -> 11%
where the time goes in v4:
time: 137 us; the launch traced here: 136 us
  starting transfers between devices  49.9 us (36%)
  blocking collectives  31.2 us (23%)
  waiting for transfers between devices  29.2 us (21%)
  Pallas kernels  20.2 us (15%)
  local copies, waits for them, and re-layouts  2.87 us (2%)
  between operations  1.67 us (1%)
    ppermute x29, starting transfers between devices, move(): return lax.ppermute(array, 'shard', pairs)  49.9 us
    ppermute x29, waiting for transfers between devices, move(): return lax.ppermute(array, 'shard', pairs)  29.2 us
    pallas_call x31, Pallas kernels, call(): pl.pallas_call(body, out_shape=[jax.ShapeDtypeStruct(s, t) for s, t in ou...  20.2 us
    all_to_all x1, blocking collectives, local(): lax.all_to_all(stepped, 'worker', split_axis=1, concat_axis=0, tiled=True)  19.9 us
    all_to_all x1, blocking collectives, local(): lax.all_to_all(spread, 'worker', split_axis=0, concat_axis=1, tiled=True)  11.3 us
  transfers between devices with their start and end apart: 29, of which 14 were waited for; matrix products, arithmetic and copies ran while one was open for 0% of the time, Pallas kernels for 11%

profile of v4, /device:TPU:64, one launch (start us, length us, event | category | flops | bytes accessed | tf_op | source)
XLA Modules:
  0.0 136.0 jit_solution(8454805565099215451)
XLA Ops:
  2.0 1.8 %pick.1 = (bf16[512,512]{1,0:T(8,128)(2,1)S(1)}, bf16[512,512]{1,0:T(8,128)(2,1)S(1)}) custom-call(bf16[512,1024]{1,0:T(8,128)(2,1)S(1)} %copy-done.3), custom_call_target="tpu_custom_call" | custom-call | flops 49999998976 | bytes 500000000 | tf_op jit(solution)/shard_map/pick/pallas_call | solution.py:67
  4.3 3.2 %product.5 = (bf16[512,2048]{1,0:T(8,128)(2,1)S(1)}, bf16[512,2048]{1,0:T(8,128)(2,1)S(1)}) custom-call(bf16[512,512]{1,0:T(8,128)(2,1)S(1)} %get-tuple-element.23.refs_0_.refs_1_, bf16[512,512]{1,0:T(8,128)(2,1)S(1)} %get-tuple-element.23.refs_0_.refs_1_, bf16[512,512]{1,0:T(8,128)(2,1)S(1)} %get-tuple-element.24.refs_2_, bf16[512,8192]{1,0:T(8,128)(2,1)S(1)} %copy-done.2), custom_call_target="tpu_custom_call" | custom-call | flops 49999998976 | bytes 500000000 | tf_op jit(solution)/shard_map/product/pallas_call | solution.py:67
  7.7 3.2 %product.6 = (bf16[512,2048]{1,0:T(8,128)(2,1)S(1)}, bf16[512,2048]{1,0:T(8,128)(2,1)S(1)}) custom-call(bf16[512,2048]{1,0:T(8,128)(2,1)S(1)} %get-tuple-element.25.refs_0_.refs_1_, bf16[512,512]{1,0:T(8,128)(2,1)S(1)} %get-tuple-element.23.refs_0_.refs_1_, bf16[512,512]{1,0:T(8,128)(2,1)S(1)} %get-tuple-element.24.refs_2_, bf16[512,8192]{1,0:T(8,128)(2,1)S(1)} %copy-done.2), custom_call_target="tpu_custom_call" | custom-call | flops 49999998976 | bytes 500000000 | tf_op jit(solution)/shard_map/product/pallas_call | solution.py:67
  11.9 2.4 %product.7 = (bf16[512,1536]{1,0:T(8,128)(2,1)S(1)}, bf16[512,1536]{1,0:T(8,128)(2,1)S(1)}) custom-call(bf16[128,2048]{1,0:T(8,128)(2,1)S(1)} %relay.19.refs_0_, bf16[512,512]{1,0:T(8,128)(2,1)S(1)} %get-tuple-element.23.refs_0_.refs_1_, bf16[512,512]{1,0:T(8,128)(2,1)S(1)} %get-tuple-element.24.refs_2_, bf16[512,8192]{1,0:T(8,128)(2,1)S(1)} %copy-done.2), custom_call_target="tpu_custom_call" | custom-call | flops 49999998976 | bytes 500000000 | tf_op jit(solution)/shard_map/product/pallas_call | solution.py:67
  18.0 2.4 %product.8 = (bf16[512,1536]{1,0:T(8,128)(2,1)S(1)}, bf16[512,1536]{1,0:T(8,128)(2,1)S(1)}) custom-call(bf16[128,1536]{1,0:T(8,128)(2,1)S(1)} %relay.21.refs_0_, bf16[512,512]{1,0:T(8,128)(2,1)S(1)} %get-tuple-element.23.refs_0_.refs_1_, bf16[512,512]{1,0:T(8,128)(2,1)S(1)} %get-tuple-element.24.refs_2_, bf16[512,8192]{1,0:T(8,128)(2,1)S(1)} %copy-done.2), custom_call_target="tpu_custom_call" | custom-call | flops 49999998976 | bytes 500000000 | tf_op jit(solution)/shard_map/product/pallas_call | solution.py:67
  20.4 4.7 %collective-permute-start.5 = (bf16[128,1536]{1,0:T(8,128)(2,1)S(1)}, bf16[128,1536]{1,0:T(8,128)(2,1)S(1)}, u32[]{:S(2)}, u32[]{:S(2)}) collective-permute-start(bf16[128,1536]{1,0:T(8,128)(2,1)S(1)} %relay.21.refs_0_), channel_id=1, source_target_pairs={{0,8},{1,25},{2,10},{3,27},{4,12},{5,29},{6,14},{7,31},{8,16},{9,1... | collective-permute-start | bytes 1179656 | tf_op jit(solution)/shard_map/ppermute | solution.py:45
  28.6 2.0 %collective-permute-done.4.refs_3_ = bf16[128,2048]{1,0:T(8,128)(2,1)S(1)} collective-permute-done((bf16[128,2048]{1,0:T(8,128)(2,1)S(1)}, bf16[128,2048]{1,0:T(8,128)(2,1)S(1)}, u32[]{:S(2)}, u32[]{:S(2)}) %collective-permute-start.4) | collective-permute-done | bytes 524320 | tf_op jit(solution)/shard_map/ppermute | solution.py:45
  31.2 1.7 %collective-permute-start.10 = (bf16[512,1024]{1,0:T(8,128)(2,1)S(1)}, bf16[512,1024]{1,0:T(8,128)(2,1)S(1)}, u32[]{:S(2)}, u32[]{:S(2)}) collective-permute-start(bf16[512,1024]{1,0:T(8,128)(2,1)S(1)} %get-tuple-element.34), channel_id=1, source_target_pairs={{0,1},{1,0},{2,3},{3,2},{4,5},{5,4},{6,7},{7,6},{8,9},{9,8},{10,11... | collective-permute-start | bytes 3145736 | tf_op jit(solution)/shard_map/ppermute | solution.py:45
  34.7 4.7 %collective-permute-start.9 = (bf16[128,1536]{1,0:T(8,128)(2,1)S(1)}, bf16[128,1536]{1,0:T(8,128)(2,1)S(1)}, u32[]{:S(2)}, u32[]{:S(2)}) collective-permute-start(bf16[128,1536]{1,0:T(8,128)(2,1)S(1)} %relay.24.refs_0_), channel_id=1, source_target_pairs={{0,8},{1,25},{2,10},{3,27},{4,12},{5,29},{6,14},{7,31},{8,16},{9,1... | collective-permute-start | bytes 1179656 | tf_op jit(solution)/shard_map/ppermute | solution.py:45
  41.2 1.9 %collective-permute-done.7.refs_3_ = bf16[128,2048]{1,0:T(8,128)(2,1)S(1)} collective-permute-done((bf16[128,2048]{1,0:T(8,128)(2,1)S(1)}, bf16[128,2048]{1,0:T(8,128)(2,1)S(1)}, u32[]{:S(2)}, u32[]{:S(2)}) %collective-permute-start.7) | collective-permute-done | bytes 524320 | tf_op jit(solution)/shard_map/ppermute | solution.py:45
  45.4 3.0 %collective-permute-done.9.refs_3_ = bf16[128,1536]{1,0:T(8,128)(2,1)S(1)} collective-permute-done((bf16[128,1536]{1,0:T(8,128)(2,1)S(1)}, bf16[128,1536]{1,0:T(8,128)(2,1)S(1)}, u32[]{:S(2)}, u32[]{:S(2)}) %collective-permute-start.9) | collective-permute-done | bytes 393248 | tf_op jit(solution)/shard_map/ppermute | solution.py:45
  48.5 4.7 %collective-permute-start.15 = (bf16[128,1536]{1,0:T(8,128)(2,1)S(1)}, bf16[128,1536]{1,0:T(8,128)(2,1)S(1)}, u32[]{:S(2)}, u32[]{:S(2)}) collective-permute-start(bf16[128,1536]{1,0:T(8,128)(2,1)S(1)} %relay.28.refs_0_), channel_id=1, source_target_pairs={{0,8},{1,25},{2,10},{3,27},{4,12},{5,29},{6,14},{7,31},{8,16},{9,1... | collective-permute-start | bytes 1179656 | tf_op jit(solution)/shard_map/ppermute | solution.py:45
  56.1 1.9 %collective-permute-start.16 = (bf16[32,4096]{1,0:T(8,128)(2,1)S(1)}, bf16[32,4096]{1,0:T(8,128)(2,1)S(1)}, u32[]{:S(2)}, u32[]{:S(2)}) collective-permute-start(bf16[32,4096]{1,0:T(8,128)(2,1)S(1)} %get-tuple-element.35.refs_0_), channel_id=1, source_target_pairs={{0,8},{1,25},{2,10},{3,27},{4,12},{5,29},{6,14},{7,31},{8,16},{9,1... | collective-permute-start | bytes 786440 | tf_op jit(solution)/shard_map/ppermute | solution.py:45
  58.0 1.9 %collective-permute-done.13.refs_3_ = bf16[128,1536]{1,0:T(8,128)(2,1)S(1)} collective-permute-done((bf16[128,1536]{1,0:T(8,128)(2,1)S(1)}, bf16[128,1536]{1,0:T(8,128)(2,1)S(1)}, u32[]{:S(2)}, u32[]{:S(2)}) %collective-permute-start.13) | collective-permute-done | bytes 393248 | tf_op jit(solution)/shard_map/ppermute | solution.py:45
  60.4 2.3 %collective-permute-done.14.refs_3_ = bf16[128,1024]{1,0:T(8,128)(2,1)S(1)} collective-permute-done((bf16[128,1024]{1,0:T(8,128)(2,1)S(1)}, bf16[128,1024]{1,0:T(8,128)(2,1)S(1)}, u32[]{:S(2)}, u32[]{:S(2)}) %collective-permute-start.14) | collective-permute-done | bytes 262176 | tf_op jit(solution)/shard_map/ppermute | solution.py:45
  65.2 2.0 %collective-permute-done.16.refs_2_ = bf16[32,4096]{1,0:T(8,128)(2,1)S(1)} collective-permute-done((bf16[32,4096]{1,0:T(8,128)(2,1)S(1)}, bf16[32,4096]{1,0:T(8,128)(2,1)S(1)}, u32[]{:S(2)}, u32[]{:S(2)}) %collective-permute-start.16) | collective-permute-done | bytes 262176 | tf_op jit(solution)/shard_map/ppermute | solution.py:45
  67.3 4.7 %collective-permute-start.20 = (bf16[32,4096]{1,0:T(8,128)(2,1)S(1)}, bf16[32,4096]{1,0:T(8,128)(2,1)S(1)}, u32[]{:S(2)}, u32[]{:S(2)}) collective-permute-start(bf16[32,4096]{1,0:T(8,128)(2,1)S(1)} %relay.32.refs_0_), channel_id=1, source_target_pairs={{0,8},{1,25},{2,10},{3,27},{4,12},{5,29},{6,14},{7,31},{8,16},{9,1... | collective-permute-start | bytes 786440 | tf_op jit(solution)/shard_map/ppermute | solution.py:45
  77.5 4.7 %collective-permute-start.24 = (bf16[32,4096]{1,0:T(8,128)(2,1)S(1)}, bf16[32,4096]{1,0:T(8,128)(2,1)S(1)}, u32[]{:S(2)}, u32[]{:S(2)}) collective-permute-start(bf16[32,4096]{1,0:T(8,128)(2,1)S(1)} %relay.36.refs_0_), channel_id=1, source_target_pairs={{0,8},{1,25},{2,10},{3,27},{4,12},{5,29},{6,14},{7,31},{8,16},{9,1... | collective-permute-start | bytes 786440 | tf_op jit(solution)/shard_map/ppermute | solution.py:45
  85.3 2.4 %collective-permute-start.27 = (bf16[32,2560]{1,0:T(8,128)(2,1)S(1)}, bf16[32,2560]{1,0:T(8,128)(2,1)S(1)}, u32[]{:S(2)}, u32[]{:S(2)}) collective-permute-start(bf16[32,2560]{1,0:T(8,128)(2,1)S(1)} %get-tuple-element.41), channel_id=1, source_target_pairs={{0,16},{1,17},{2,18},{3,19},{4,20},{5,21},{6,22},{7,23},{8,24},{9,... | collective-permute-start | bytes 491528 | tf_op jit(solution)/shard_map/ppermute | solution.py:45
  87.7 1.7 %collective-permute-start.28 = (bf16[32,2560]{1,0:T(8,128)(2,1)S(1)}, bf16[32,2560]{1,0:T(8,128)(2,1)S(1)}, u32[]{:S(2)}, u32[]{:S(2)}) collective-permute-start(bf16[32,2560]{1,0:T(8,128)(2,1)S(1)} %get-tuple-element.42), channel_id=1, source_target_pairs={{0,8},{1,25},{2,10},{3,27},{4,12},{5,29},{6,14},{7,31},{8,16},{9,1... | collective-permute-start | bytes 491528 | tf_op jit(solution)/shard_map/ppermute | solution.py:45
  89.5 4.9 %collective-permute-done.24.refs_6_ = bf16[32,4096]{1,0:T(8,128)(2,1)S(1)} collective-permute-done((bf16[32,4096]{1,0:T(8,128)(2,1)S(1)}, bf16[32,4096]{1,0:T(8,128)(2,1)S(1)}, u32[]{:S(2)}, u32[]{:S(2)}) %collective-permute-start.24) | collective-permute-done | bytes 262176 | tf_op jit(solution)/shard_map/ppermute | solution.py:45
  96.1 5.9 %collective-permute-done.26.refs_6_ = bf16[32,2560]{1,0:T(8,128)(2,1)S(1)} collective-permute-done((bf16[32,2560]{1,0:T(8,128)(2,1)S(1)}, bf16[32,2560]{1,0:T(8,128)(2,1)S(1)}, u32[]{:S(2)}, u32[]{:S(2)}) %collective-permute-start.26) | collective-permute-done | bytes 163872 | tf_op jit(solution)/shard_map/ppermute | solution.py:45
  103.1 19.9 %all_to_all.29 = f32[32,8,1024]{2,0,1:T(8,128)S(1)} all-to-all(f32[32,8,1024]{2,0,1:T(8,128)S(1)} %bitcast.20), channel_id=1, replica_groups=mesh['worker'=8,'shard'=32] {'worker'}, dimensions={1} | all-to-all | bytes 2097152 | tf_op jit(solution)/shard_map/all_to_all | solution.py:280
  123.9 11.3 %all_to_all.30 = bf16[8,32,1024]{2,1,0:T(8,128)(2,1)S(1)} all-to-all(bf16[8,32,1024]{2,1,0:T(8,128)(2,1)S(1)} %broadcast_in_dim.2), channel_id=1, replica_groups=mesh['worker'=8,'shard'=32] {'worker'}, dimensions={0} | all-to-all | bytes 1048576 | tf_op jit(solution)/shard_map/all_to_all | solution.py:286
  (92 shorter events, 35.0 us)
Async XLA Ops:
  14.6 12.2 %collective-permute-start.3 = (bf16[128,2048]{1,0:T(8,128)(2,1)S(1)}, bf16[128,2048]{1,0:T(8,128)(2,1)S(1)}, u32[]{:S(2)}, u32[]{:S(2)}) collective-permute-start(bf16[128,2048]{1,0:T(8,128)(2,1)S(1)} %relay.19.refs_0_), channel_id=1, source_target_pairs={{0,2},{1,7},{2,4},{3,1},{4,6},{5,3},{6,0},{7,5},{8,10},{9,15},{10,... | collective-permute-start | bytes 1572872 | tf_op jit(solution)/shard_map/ppermute | solution.py:45
  16.3 14.3 %collective-permute-start.4 = (bf16[128,2048]{1,0:T(8,128)(2,1)S(1)}, bf16[128,2048]{1,0:T(8,128)(2,1)S(1)}, u32[]{:S(2)}, u32[]{:S(2)}) collective-permute-start(bf16[128,2048]{1,0:T(8,128)(2,1)S(1)} %relay.20.refs_0_), channel_id=1, source_target_pairs={{0,2},{1,7},{2,4},{3,1},{4,6},{5,3},{6,0},{7,5},{8,10},{9,15},{10,... | collective-permute-start | bytes 1572872 | tf_op jit(solution)/shard_map/ppermute | solution.py:45
  20.4 14.2 %collective-permute-start.5 = (bf16[128,1536]{1,0:T(8,128)(2,1)S(1)}, bf16[128,1536]{1,0:T(8,128)(2,1)S(1)}, u32[]{:S(2)}, u32[]{:S(2)}) collective-permute-start(bf16[128,1536]{1,0:T(8,128)(2,1)S(1)} %relay.21.refs_0_), channel_id=1, source_target_pairs={{0,8},{1,25},{2,10},{3,27},{4,12},{5,29},{6,14},{7,31},{8,16},{9,1... | collective-permute-start | bytes 1179656 | tf_op jit(solution)/shard_map/ppermute | solution.py:45
  25.2 18.5 %collective-permute-start.8 = (bf16[512,1536]{1,0:T(8,128)(2,1)S(1)}, bf16[512,1536]{1,0:T(8,128)(2,1)S(1)}, u32[]{:S(2)}, u32[]{:S(2)}) collective-permute-start(bf16[512,1536]{1,0:T(8,128)(2,1)S(1)} %get-tuple-element.33), channel_id=1, source_target_pairs={{0,1},{1,0},{2,3},{3,2},{4,5},{5,4},{6,7},{7,6},{8,9},{9,8},{10,11... | collective-permute-start | bytes 4718600 | tf_op jit(solution)/shard_map/ppermute | solution.py:45
  27.0 12.4 %collective-permute-start.6 = (bf16[128,2048]{1,0:T(8,128)(2,1)S(1)}, bf16[128,2048]{1,0:T(8,128)(2,1)S(1)}, u32[]{:S(2)}, u32[]{:S(2)}) collective-permute-start(bf16[128,2048]{1,0:T(8,128)(2,1)S(1)} %relay.22.refs_0_), channel_id=1, source_target_pairs={{0,2},{1,7},{2,4},{3,1},{4,6},{5,3},{6,0},{7,5},{8,10},{9,15},{10,... | collective-permute-start | bytes 1572872 | tf_op jit(solution)/shard_map/ppermute | solution.py:45
  30.8 12.3 %collective-permute-start.7 = (bf16[128,2048]{1,0:T(8,128)(2,1)S(1)}, bf16[128,2048]{1,0:T(8,128)(2,1)S(1)}, u32[]{:S(2)}, u32[]{:S(2)}) collective-permute-start(bf16[128,2048]{1,0:T(8,128)(2,1)S(1)} %relay.23.refs_0_), channel_id=1, source_target_pairs={{0,2},{1,7},{2,4},{3,1},{4,6},{5,3},{6,0},{7,5},{8,10},{9,15},{10,... | collective-permute-start | bytes 1572872 | tf_op jit(solution)/shard_map/ppermute | solution.py:45
  31.2 22.0 %collective-permute-start.10 = (bf16[512,1024]{1,0:T(8,128)(2,1)S(1)}, bf16[512,1024]{1,0:T(8,128)(2,1)S(1)}, u32[]{:S(2)}, u32[]{:S(2)}) collective-permute-start(bf16[512,1024]{1,0:T(8,128)(2,1)S(1)} %get-tuple-element.34), channel_id=1, source_target_pairs={{0,1},{1,0},{2,3},{3,2},{4,5},{5,4},{6,7},{7,6},{8,9},{9,8},{10,11... | collective-permute-start | bytes 3145736 | tf_op jit(solution)/shard_map/ppermute | solution.py:45
  34.7 13.6 %collective-permute-start.9 = (bf16[128,1536]{1,0:T(8,128)(2,1)S(1)}, bf16[128,1536]{1,0:T(8,128)(2,1)S(1)}, u32[]{:S(2)}, u32[]{:S(2)}) collective-permute-start(bf16[128,1536]{1,0:T(8,128)(2,1)S(1)} %relay.24.refs_0_), channel_id=1, source_target_pairs={{0,8},{1,25},{2,10},{3,27},{4,12},{5,29},{6,14},{7,31},{8,16},{9,1... | collective-permute-start | bytes 1179656 | tf_op jit(solution)/shard_map/ppermute | solution.py:45
  39.6 16.1 %collective-permute-start.11 = (bf16[128,2048]{1,0:T(8,128)(2,1)S(1)}, bf16[128,2048]{1,0:T(8,128)(2,1)S(1)}, u32[]{:S(2)}, u32[]{:S(2)}) collective-permute-start(bf16[128,2048]{1,0:T(8,128)(2,1)S(1)} %relay.25.refs_0_), channel_id=1, source_target_pairs={{0,2},{1,7},{2,4},{3,1},{4,6},{5,3},{6,0},{7,5},{8,10},{9,15},{10,... | collective-permute-start | bytes 1572872 | tf_op jit(solution)/shard_map/ppermute | solution.py:45
  43.3 12.4 %collective-permute-start.12 = (bf16[128,2048]{1,0:T(8,128)(2,1)S(1)}, bf16[128,2048]{1,0:T(8,128)(2,1)S(1)}, u32[]{:S(2)}, u32[]{:S(2)}) collective-permute-start(bf16[128,2048]{1,0:T(8,128)(2,1)S(1)} %relay.26.refs_0_), channel_id=1, source_target_pairs={{0,2},{1,7},{2,4},{3,1},{4,6},{5,3},{6,0},{7,5},{8,10},{9,15},{10,... | collective-permute-start | bytes 1572872 | tf_op jit(solution)/shard_map/ppermute | solution.py:45
  43.8 16.1 %collective-permute-start.13 = (bf16[128,1536]{1,0:T(8,128)(2,1)S(1)}, bf16[128,1536]{1,0:T(8,128)(2,1)S(1)}, u32[]{:S(2)}, u32[]{:S(2)}) collective-permute-start(bf16[128,1536]{1,0:T(8,128)(2,1)S(1)} %relay.27.refs_0_), channel_id=1, source_target_pairs={{0,2},{1,7},{2,4},{3,1},{4,6},{5,3},{6,0},{7,5},{8,10},{9,15},{10,... | collective-permute-start | bytes 1179656 | tf_op jit(solution)/shard_map/ppermute | solution.py:45
  48.5 14.9 %collective-permute-start.15 = (bf16[128,1536]{1,0:T(8,128)(2,1)S(1)}, bf16[128,1536]{1,0:T(8,128)(2,1)S(1)}, u32[]{:S(2)}, u32[]{:S(2)}) collective-permute-start(bf16[128,1536]{1,0:T(8,128)(2,1)S(1)} %relay.28.refs_0_), channel_id=1, source_target_pairs={{0,8},{1,25},{2,10},{3,27},{4,12},{5,29},{6,14},{7,31},{8,16},{9,1... | collective-permute-start | bytes 1179656 | tf_op jit(solution)/shard_map/ppermute | solution.py:45
  53.3 9.5 %collective-permute-start.14 = (bf16[128,1024]{1,0:T(8,128)(2,1)S(1)}, bf16[128,1024]{1,0:T(8,128)(2,1)S(1)}, u32[]{:S(2)}, u32[]{:S(2)}) collective-permute-start(bf16[128,1024]{1,0:T(8,128)(2,1)S(1)} %relay.29.refs_0_), channel_id=1, source_target_pairs={{0,2},{1,7},{2,4},{3,1},{4,6},{5,3},{6,0},{7,5},{8,10},{9,15},{10,... | collective-permute-start | bytes 786440 | tf_op jit(solution)/shard_map/ppermute | solution.py:45
  56.1 11.1 %collective-permute-start.16 = (bf16[32,4096]{1,0:T(8,128)(2,1)S(1)}, bf16[32,4096]{1,0:T(8,128)(2,1)S(1)}, u32[]{:S(2)}, u32[]{:S(2)}) collective-permute-start(bf16[32,4096]{1,0:T(8,128)(2,1)S(1)} %get-tuple-element.35.refs_0_), channel_id=1, source_target_pairs={{0,8},{1,25},{2,10},{3,27},{4,12},{5,29},{6,14},{7,31},{8,16},{9,1... | collective-permute-start | bytes 786440 | tf_op jit(solution)/shard_map/ppermute | solution.py:45
  60.1 11.9 %collective-permute-start.17 = (bf16[128,1536]{1,0:T(8,128)(2,1)S(1)}, bf16[128,1536]{1,0:T(8,128)(2,1)S(1)}, u32[]{:S(2)}, u32[]{:S(2)}) collective-permute-start(bf16[128,1536]{1,0:T(8,128)(2,1)S(1)} %relay.30.refs_0_), channel_id=1, source_target_pairs={{0,2},{1,7},{2,4},{3,1},{4,6},{5,3},{6,0},{7,5},{8,10},{9,15},{10,... | collective-permute-start | bytes 1179656 | tf_op jit(solution)/shard_map/ppermute | solution.py:45
  62.8 11.7 %collective-permute-start.19 = (bf16[128,1024]{1,0:T(8,128)(2,1)S(1)}, bf16[128,1024]{1,0:T(8,128)(2,1)S(1)}, u32[]{:S(2)}, u32[]{:S(2)}) collective-permute-start(bf16[128,1024]{1,0:T(8,128)(2,1)S(1)} %relay.31.refs_0_), channel_id=1, source_target_pairs={{0,2},{1,7},{2,4},{3,1},{4,6},{5,3},{6,0},{7,5},{8,10},{9,15},{10,... | collective-permute-start | bytes 786440 | tf_op jit(solution)/shard_map/ppermute | solution.py:45
  67.3 10.2 %collective-permute-start.20 = (bf16[32,4096]{1,0:T(8,128)(2,1)S(1)}, bf16[32,4096]{1,0:T(8,128)(2,1)S(1)}, u32[]{:S(2)}, u32[]{:S(2)}) collective-permute-start(bf16[32,4096]{1,0:T(8,128)(2,1)S(1)} %relay.32.refs_0_), channel_id=1, source_target_pairs={{0,8},{1,25},{2,10},{3,27},{4,12},{5,29},{6,14},{7,31},{8,16},{9,1... | collective-permute-start | bytes 786440 | tf_op jit(solution)/shard_map/ppermute | solution.py:45
  72.1 12.9 %collective-permute-start.22 = (bf16[128,1536]{1,0:T(8,128)(2,1)S(1)}, bf16[128,1536]{1,0:T(8,128)(2,1)S(1)}, u32[]{:S(2)}, u32[]{:S(2)}) collective-permute-start(bf16[128,1536]{1,0:T(8,128)(2,1)S(1)} %relay.33.refs_0_), channel_id=1, source_target_pairs={{0,2},{1,7},{2,4},{3,1},{4,6},{5,3},{6,0},{7,5},{8,10},{9,15},{10,... | collective-permute-start | bytes 1179656 | tf_op jit(solution)/shard_map/ppermute | solution.py:45
  74.6 10.4 %collective-permute-start.23 = (bf16[128,1024]{1,0:T(8,128)(2,1)S(1)}, bf16[128,1024]{1,0:T(8,128)(2,1)S(1)}, u32[]{:S(2)}, u32[]{:S(2)}) collective-permute-start(bf16[128,1024]{1,0:T(8,128)(2,1)S(1)} %relay.35.refs_0_), channel_id=1, source_target_pairs={{0,2},{1,7},{2,4},{3,1},{4,6},{5,3},{6,0},{7,5},{8,10},{9,15},{10,... | collective-permute-start | bytes 786440 | tf_op jit(solution)/shard_map/ppermute | solution.py:45
  77.5 16.8 %collective-permute-start.24 = (bf16[32,4096]{1,0:T(8,128)(2,1)S(1)}, bf16[32,4096]{1,0:T(8,128)(2,1)S(1)}, u32[]{:S(2)}, u32[]{:S(2)}) collective-permute-start(bf16[32,4096]{1,0:T(8,128)(2,1)S(1)} %relay.36.refs_0_), channel_id=1, source_target_pairs={{0,8},{1,25},{2,10},{3,27},{4,12},{5,29},{6,14},{7,31},{8,16},{9,1... | collective-permute-start | bytes 786440 | tf_op jit(solution)/shard_map/ppermute | solution.py:45
  82.3 13.1 %collective-permute-start.25 = (bf16[32,1536]{1,0:T(8,128)(2,1)S(1)}, bf16[32,1536]{1,0:T(8,128)(2,1)S(1)}, u32[]{:S(2)}, u32[]{:S(2)}) collective-permute-start(bf16[32,1536]{1,0:T(8,128)(2,1)S(1)} %relay.37.refs_0_), channel_id=1, source_target_pairs={{0,2},{1,7},{2,4},{3,1},{4,6},{5,3},{6,0},{7,5},{8,10},{9,15},{10,... | collective-permute-start | bytes 294920 | tf_op jit(solution)/shard_map/ppermute | solution.py:45
  85.3 16.7 %collective-permute-start.26 = (bf16[32,2560]{1,0:T(8,128)(2,1)S(1)}, bf16[32,2560]{1,0:T(8,128)(2,1)S(1)}, u32[]{:S(2)}, u32[]{:S(2)}) collective-permute-start(bf16[32,2560]{1,0:T(8,128)(2,1)S(1)} %get-tuple-element.39.refs_0_), channel_id=1, source_target_pairs={{0,24},{1,9},{2,26},{3,11},{4,28},{5,13},{6,30},{7,15},{8,0},{9,17... | collective-permute-start | bytes 491528 | tf_op jit(solution)/shard_map/ppermute | solution.py:45
  85.3 16.7 %collective-permute-start.27 = (bf16[32,2560]{1,0:T(8,128)(2,1)S(1)}, bf16[32,2560]{1,0:T(8,128)(2,1)S(1)}, u32[]{:S(2)}, u32[]{:S(2)}) collective-permute-start(bf16[32,2560]{1,0:T(8,128)(2,1)S(1)} %get-tuple-element.41), channel_id=1, source_target_pairs={{0,16},{1,17},{2,18},{3,19},{4,20},{5,21},{6,22},{7,23},{8,24},{9,... | collective-permute-start | bytes 491528 | tf_op jit(solution)/shard_map/ppermute | solution.py:45
  87.7 14.3 %collective-permute-start.28 = (bf16[32,2560]{1,0:T(8,128)(2,1)S(1)}, bf16[32,2560]{1,0:T(8,128)(2,1)S(1)}, u32[]{:S(2)}, u32[]{:S(2)}) collective-permute-start(bf16[32,2560]{1,0:T(8,128)(2,1)S(1)} %get-tuple-element.42), channel_id=1, source_target_pairs={{0,8},{1,25},{2,10},{3,27},{4,12},{5,29},{6,14},{7,31},{8,16},{9,1... | collective-permute-start | bytes 491528 | tf_op jit(solution)/shard_map/ppermute | solution.py:45
  (14 other events, 118.9 us)

commit v5 on v3

--- a/solution.py
+++ b/solution.py
@@ -265,9 +265,9 @@
     run("relay", relay("d", "y"))
     run("settle", settle("e", "y"))
     run("relay", relay("ab", "z"))
-    run("relay", relay("e", "y"), cost=LATE_COST)
     run("relay", relay("c", "y"), cost=LATE_COST)
     run("relay", relay("d", "y"), cost=LATE_COST)
+    run("relay", relay("e", "y"))
     run("relay", relay("ab", "z"), cost=LATE_COST)
     run("relay", relay("e", "y"))
     run("settle", settle("cd", "z", direct=True))

time: 140 us -> 139 us (level)
  starting transfers between devices: 52.4 us -> 48.4 us
  blocking collectives: 32.4 us -> 34.4 us
  waiting for transfers between devices: 28.6 us -> 30.5 us
    ppermute x29, starting transfers between devices: 52.4 us -> 48.4 us  [move(): return lax.ppermute(array, 'shard', pairs)]
    all_to_all x1, blocking collectives: 12.2 us -> 14.2 us  [local(): lax.all_to_all(spread, 'worker', split_axis=0, concat_axis=1, tiled=True)]
    ppermute x29, waiting for transfers between devices: 28.6 us -> 30.5 us  [move(): return lax.ppermute(array, 'shard', pairs)]
  transfers between devices with their start and end apart: 29 -> 29, of which waited for: 13 -> 14; matrix products, arithmetic and copies ran while one was open for 0% -> 0% of each run, Pallas kernels for 10% -> 10%
where the time goes in v5:
time: 139 us
  starting transfers between devices  48.4 us (35%)
  blocking collectives  34.4 us (25%)
  waiting for transfers between devices  30.5 us (22%)
  Pallas kernels  20.2 us (15%)
  local copies, waits for them, and re-layouts  2.87 us (2%)
  between operations  1.7 us (1%)
    ppermute x29, starting transfers between devices, move(): return lax.ppermute(array, 'shard', pairs)  48.4 us
    ppermute x29, waiting for transfers between devices, move(): return lax.ppermute(array, 'shard', pairs)  30.5 us
    pallas_call x31, Pallas kernels, call(): pl.pallas_call(body, out_shape=[jax.ShapeDtypeStruct(s, t) for s, t in ou...  20.2 us
    all_to_all x1, blocking collectives, local(): lax.all_to_all(stepped, 'worker', split_axis=1, concat_axis=0, tiled=True)  20.2 us
    all_to_all x1, blocking collectives, local(): lax.all_to_all(spread, 'worker', split_axis=0, concat_axis=1, tiled=True)  14.2 us
  transfers between devices with their start and end apart: 29, of which 14 were waited for; matrix products, arithmetic and copies ran while one was open for 0% of the time, Pallas kernels for 10%

profile of v5, /device:TPU:64, one launch (start us, length us, event | category | flops | bytes accessed | tf_op | source)
XLA Modules:
  0.0 139.1 jit_solution(8325098057563200579)
XLA Ops:
  2.0 1.8 %pick.1 = (bf16[512,512]{1,0:T(8,128)(2,1)S(1)}, bf16[512,512]{1,0:T(8,128)(2,1)S(1)}) custom-call(bf16[512,1024]{1,0:T(8,128)(2,1)S(1)} %copy-done.3), custom_call_target="tpu_custom_call" | custom-call | flops 49999998976 | bytes 500000000 | tf_op jit(solution)/shard_map/pick/pallas_call | solution.py:67
  4.3 3.2 %product.5 = (bf16[512,2048]{1,0:T(8,128)(2,1)S(1)}, bf16[512,2048]{1,0:T(8,128)(2,1)S(1)}) custom-call(bf16[512,512]{1,0:T(8,128)(2,1)S(1)} %get-tuple-element.23.refs_0_.refs_1_, bf16[512,512]{1,0:T(8,128)(2,1)S(1)} %get-tuple-element.23.refs_0_.refs_1_, bf16[512,512]{1,0:T(8,128)(2,1)S(1)} %get-tuple-element.24.refs_2_, bf16[512,8192]{1,0:T(8,128)(2,1)S(1)} %copy-done.2), custom_call_target="tpu_custom_call" | custom-call | flops 49999998976 | bytes 500000000 | tf_op jit(solution)/shard_map/product/pallas_call | solution.py:67
  7.7 3.2 %product.6 = (bf16[512,2048]{1,0:T(8,128)(2,1)S(1)}, bf16[512,2048]{1,0:T(8,128)(2,1)S(1)}) custom-call(bf16[512,2048]{1,0:T(8,128)(2,1)S(1)} %get-tuple-element.25.refs_0_.refs_1_, bf16[512,512]{1,0:T(8,128)(2,1)S(1)} %get-tuple-element.23.refs_0_.refs_1_, bf16[512,512]{1,0:T(8,128)(2,1)S(1)} %get-tuple-element.24.refs_2_, bf16[512,8192]{1,0:T(8,128)(2,1)S(1)} %copy-done.2), custom_call_target="tpu_custom_call" | custom-call | flops 49999998976 | bytes 500000000 | tf_op jit(solution)/shard_map/product/pallas_call | solution.py:67
  11.9 2.4 %product.7 = (bf16[512,1536]{1,0:T(8,128)(2,1)S(1)}, bf16[512,1536]{1,0:T(8,128)(2,1)S(1)}) custom-call(bf16[128,2048]{1,0:T(8,128)(2,1)S(1)} %relay.19.refs_0_, bf16[512,512]{1,0:T(8,128)(2,1)S(1)} %get-tuple-element.23.refs_0_.refs_1_, bf16[512,512]{1,0:T(8,128)(2,1)S(1)} %get-tuple-element.24.refs_2_, bf16[512,8192]{1,0:T(8,128)(2,1)S(1)} %copy-done.2), custom_call_target="tpu_custom_call" | custom-call | flops 49999998976 | bytes 500000000 | tf_op jit(solution)/shard_map/product/pallas_call | solution.py:67
  18.0 2.4 %product.8 = (bf16[512,1536]{1,0:T(8,128)(2,1)S(1)}, bf16[512,1536]{1,0:T(8,128)(2,1)S(1)}) custom-call(bf16[128,1536]{1,0:T(8,128)(2,1)S(1)} %relay.21.refs_0_, bf16[512,512]{1,0:T(8,128)(2,1)S(1)} %get-tuple-element.23.refs_0_.refs_1_, bf16[512,512]{1,0:T(8,128)(2,1)S(1)} %get-tuple-element.24.refs_2_, bf16[512,8192]{1,0:T(8,128)(2,1)S(1)} %copy-done.2), custom_call_target="tpu_custom_call" | custom-call | flops 49999998976 | bytes 500000000 | tf_op jit(solution)/shard_map/product/pallas_call | solution.py:67
  20.4 4.7 %collective-permute-start.5 = (bf16[128,1536]{1,0:T(8,128)(2,1)S(1)}, bf16[128,1536]{1,0:T(8,128)(2,1)S(1)}, u32[]{:S(2)}, u32[]{:S(2)}) collective-permute-start(bf16[128,1536]{1,0:T(8,128)(2,1)S(1)} %relay.21.refs_0_), channel_id=1, source_target_pairs={{0,8},{1,25},{2,10},{3,27},{4,12},{5,29},{6,14},{7,31},{8,16},{9,1... | collective-permute-start | bytes 1179656 | tf_op jit(solution)/shard_map/ppermute | solution.py:45
  28.6 2.0 %collective-permute-done.4.refs_3_ = bf16[128,2048]{1,0:T(8,128)(2,1)S(1)} collective-permute-done((bf16[128,2048]{1,0:T(8,128)(2,1)S(1)}, bf16[128,2048]{1,0:T(8,128)(2,1)S(1)}, u32[]{:S(2)}, u32[]{:S(2)}) %collective-permute-start.4) | collective-permute-done | bytes 524320 | tf_op jit(solution)/shard_map/ppermute | solution.py:45
  34.7 4.7 %collective-permute-start.9 = (bf16[128,1536]{1,0:T(8,128)(2,1)S(1)}, bf16[128,1536]{1,0:T(8,128)(2,1)S(1)}, u32[]{:S(2)}, u32[]{:S(2)}) collective-permute-start(bf16[128,1536]{1,0:T(8,128)(2,1)S(1)} %relay.24.refs_0_), channel_id=1, source_target_pairs={{0,8},{1,25},{2,10},{3,27},{4,12},{5,29},{6,14},{7,31},{8,16},{9,1... | collective-permute-start | bytes 1179656 | tf_op jit(solution)/shard_map/ppermute | solution.py:45
  41.2 1.9 %collective-permute-done.7.refs_3_ = bf16[128,2048]{1,0:T(8,128)(2,1)S(1)} collective-permute-done((bf16[128,2048]{1,0:T(8,128)(2,1)S(1)}, bf16[128,2048]{1,0:T(8,128)(2,1)S(1)}, u32[]{:S(2)}, u32[]{:S(2)}) %collective-permute-start.7) | collective-permute-done | bytes 524320 | tf_op jit(solution)/shard_map/ppermute | solution.py:45
  45.4 3.0 %collective-permute-done.9.refs_3_ = bf16[128,1536]{1,0:T(8,128)(2,1)S(1)} collective-permute-done((bf16[128,1536]{1,0:T(8,128)(2,1)S(1)}, bf16[128,1536]{1,0:T(8,128)(2,1)S(1)}, u32[]{:S(2)}, u32[]{:S(2)}) %collective-permute-start.9) | collective-permute-done | bytes 393248 | tf_op jit(solution)/shard_map/ppermute | solution.py:45
  48.5 4.7 %collective-permute-start.15 = (bf16[128,1536]{1,0:T(8,128)(2,1)S(1)}, bf16[128,1536]{1,0:T(8,128)(2,1)S(1)}, u32[]{:S(2)}, u32[]{:S(2)}) collective-permute-start(bf16[128,1536]{1,0:T(8,128)(2,1)S(1)} %relay.28.refs_0_), channel_id=1, source_target_pairs={{0,8},{1,25},{2,10},{3,27},{4,12},{5,29},{6,14},{7,31},{8,16},{9,1... | collective-permute-start | bytes 1179656 | tf_op jit(solution)/shard_map/ppermute | solution.py:45
  56.1 1.9 %collective-permute-start.16 = (bf16[32,4096]{1,0:T(8,128)(2,1)S(1)}, bf16[32,4096]{1,0:T(8,128)(2,1)S(1)}, u32[]{:S(2)}, u32[]{:S(2)}) collective-permute-start(bf16[32,4096]{1,0:T(8,128)(2,1)S(1)} %get-tuple-element.35.refs_0_), channel_id=1, source_target_pairs={{0,8},{1,25},{2,10},{3,27},{4,12},{5,29},{6,14},{7,31},{8,16},{9,1... | collective-permute-start | bytes 786440 | tf_op jit(solution)/shard_map/ppermute | solution.py:45
  58.0 1.9 %collective-permute-done.13.refs_3_ = bf16[128,1536]{1,0:T(8,128)(2,1)S(1)} collective-permute-done((bf16[128,1536]{1,0:T(8,128)(2,1)S(1)}, bf16[128,1536]{1,0:T(8,128)(2,1)S(1)}, u32[]{:S(2)}, u32[]{:S(2)}) %collective-permute-start.13) | collective-permute-done | bytes 393248 | tf_op jit(solution)/shard_map/ppermute | solution.py:45
  60.4 2.3 %collective-permute-done.14.refs_3_ = bf16[128,1024]{1,0:T(8,128)(2,1)S(1)} collective-permute-done((bf16[128,1024]{1,0:T(8,128)(2,1)S(1)}, bf16[128,1024]{1,0:T(8,128)(2,1)S(1)}, u32[]{:S(2)}, u32[]{:S(2)}) %collective-permute-start.14) | collective-permute-done | bytes 262176 | tf_op jit(solution)/shard_map/ppermute | solution.py:45
  65.2 2.0 %collective-permute-done.16.refs_2_ = bf16[32,4096]{1,0:T(8,128)(2,1)S(1)} collective-permute-done((bf16[32,4096]{1,0:T(8,128)(2,1)S(1)}, bf16[32,4096]{1,0:T(8,128)(2,1)S(1)}, u32[]{:S(2)}, u32[]{:S(2)}) %collective-permute-start.16) | collective-permute-done | bytes 262176 | tf_op jit(solution)/shard_map/ppermute | solution.py:45
  67.3 4.7 %collective-permute-start.20 = (bf16[32,4096]{1,0:T(8,128)(2,1)S(1)}, bf16[32,4096]{1,0:T(8,128)(2,1)S(1)}, u32[]{:S(2)}, u32[]{:S(2)}) collective-permute-start(bf16[32,4096]{1,0:T(8,128)(2,1)S(1)} %relay.32.refs_0_), channel_id=1, source_target_pairs={{0,8},{1,25},{2,10},{3,27},{4,12},{5,29},{6,14},{7,31},{8,16},{9,1... | collective-permute-start | bytes 786440 | tf_op jit(solution)/shard_map/ppermute | solution.py:45
  77.5 4.7 %collective-permute-start.24 = (bf16[32,4096]{1,0:T(8,128)(2,1)S(1)}, bf16[32,4096]{1,0:T(8,128)(2,1)S(1)}, u32[]{:S(2)}, u32[]{:S(2)}) collective-permute-start(bf16[32,4096]{1,0:T(8,128)(2,1)S(1)} %relay.36.refs_0_), channel_id=1, source_target_pairs={{0,8},{1,25},{2,10},{3,27},{4,12},{5,29},{6,14},{7,31},{8,16},{9,1... | collective-permute-start | bytes 786440 | tf_op jit(solution)/shard_map/ppermute | solution.py:45
  82.2 2.8 %collective-permute-done.21.refs_2_ = bf16[32,1536]{1,0:T(8,128)(2,1)S(1)} collective-permute-done((bf16[32,1536]{1,0:T(8,128)(2,1)S(1)}, bf16[32,1536]{1,0:T(8,128)(2,1)S(1)}, u32[]{:S(2)}, u32[]{:S(2)}) %collective-permute-start.21) | collective-permute-done | bytes 98336 | tf_op jit(solution)/shard_map/ppermute | solution.py:45
  85.5 2.4 %collective-permute-start.27 = (bf16[32,2560]{1,0:T(8,128)(2,1)S(1)}, bf16[32,2560]{1,0:T(8,128)(2,1)S(1)}, u32[]{:S(2)}, u32[]{:S(2)}) collective-permute-start(bf16[32,2560]{1,0:T(8,128)(2,1)S(1)} %get-tuple-element.41), channel_id=1, source_target_pairs={{0,16},{1,17},{2,18},{3,19},{4,20},{5,21},{6,22},{7,23},{8,24},{9,... | collective-permute-start | bytes 491528 | tf_op jit(solution)/shard_map/ppermute | solution.py:45
  87.9 1.7 %collective-permute-start.28 = (bf16[32,2560]{1,0:T(8,128)(2,1)S(1)}, bf16[32,2560]{1,0:T(8,128)(2,1)S(1)}, u32[]{:S(2)}, u32[]{:S(2)}) collective-permute-start(bf16[32,2560]{1,0:T(8,128)(2,1)S(1)} %get-tuple-element.42), channel_id=1, source_target_pairs={{0,8},{1,25},{2,10},{3,27},{4,12},{5,29},{6,14},{7,31},{8,16},{9,1... | collective-permute-start | bytes 491528 | tf_op jit(solution)/shard_map/ppermute | solution.py:45
  89.7 4.2 %collective-permute-done.24.refs_6_ = bf16[32,4096]{1,0:T(8,128)(2,1)S(1)} collective-permute-done((bf16[32,4096]{1,0:T(8,128)(2,1)S(1)}, bf16[32,4096]{1,0:T(8,128)(2,1)S(1)}, u32[]{:S(2)}, u32[]{:S(2)}) %collective-permute-start.24) | collective-permute-done | bytes 262176 | tf_op jit(solution)/shard_map/ppermute | solution.py:45
  95.6 5.7 %collective-permute-done.26.refs_6_ = bf16[32,2560]{1,0:T(8,128)(2,1)S(1)} collective-permute-done((bf16[32,2560]{1,0:T(8,128)(2,1)S(1)}, bf16[32,2560]{1,0:T(8,128)(2,1)S(1)}, u32[]{:S(2)}, u32[]{:S(2)}) %collective-permute-start.26) | collective-permute-done | bytes 163872 | tf_op jit(solution)/shard_map/ppermute | solution.py:45
  102.9 20.2 %all_to_all.29 = f32[32,8,1024]{2,0,1:T(8,128)S(1)} all-to-all(f32[32,8,1024]{2,0,1:T(8,128)S(1)} %bitcast.20), channel_id=1, replica_groups=mesh['worker'=8,'shard'=32] {'worker'}, dimensions={1} | all-to-all | bytes 2097152 | tf_op jit(solution)/shard_map/all_to_all | solution.py:280
  124.0 14.2 %all_to_all.30 = bf16[8,32,1024]{2,1,0:T(8,128)(2,1)S(1)} all-to-all(bf16[8,32,1024]{2,1,0:T(8,128)(2,1)S(1)} %broadcast_in_dim.2), channel_id=1, replica_groups=mesh['worker'=8,'shard'=32] {'worker'}, dimensions={0} | all-to-all | bytes 1048576 | tf_op jit(solution)/shard_map/all_to_all | solution.py:286
  (92 shorter events, 34.6 us)
Async XLA Ops:
  14.6 12.2 %collective-permute-start.3 = (bf16[128,2048]{1,0:T(8,128)(2,1)S(1)}, bf16[128,2048]{1,0:T(8,128)(2,1)S(1)}, u32[]{:S(2)}, u32[]{:S(2)}) collective-permute-start(bf16[128,2048]{1,0:T(8,128)(2,1)S(1)} %relay.19.refs_0_), channel_id=1, source_target_pairs={{0,2},{1,7},{2,4},{3,1},{4,6},{5,3},{6,0},{7,5},{8,10},{9,15},{10,... | collective-permute-start | bytes 1572872 | tf_op jit(solution)/shard_map/ppermute | solution.py:45
  16.3 14.3 %collective-permute-start.4 = (bf16[128,2048]{1,0:T(8,128)(2,1)S(1)}, bf16[128,2048]{1,0:T(8,128)(2,1)S(1)}, u32[]{:S(2)}, u32[]{:S(2)}) collective-permute-start(bf16[128,2048]{1,0:T(8,128)(2,1)S(1)} %relay.20.refs_0_), channel_id=1, source_target_pairs={{0,2},{1,7},{2,4},{3,1},{4,6},{5,3},{6,0},{7,5},{8,10},{9,15},{10,... | collective-permute-start | bytes 1572872 | tf_op jit(solution)/shard_map/ppermute | solution.py:45
  20.4 14.2 %collective-permute-start.5 = (bf16[128,1536]{1,0:T(8,128)(2,1)S(1)}, bf16[128,1536]{1,0:T(8,128)(2,1)S(1)}, u32[]{:S(2)}, u32[]{:S(2)}) collective-permute-start(bf16[128,1536]{1,0:T(8,128)(2,1)S(1)} %relay.21.refs_0_), channel_id=1, source_target_pairs={{0,8},{1,25},{2,10},{3,27},{4,12},{5,29},{6,14},{7,31},{8,16},{9,1... | collective-permute-start | bytes 1179656 | tf_op jit(solution)/shard_map/ppermute | solution.py:45
  25.2 18.5 %collective-permute-start.8 = (bf16[512,1536]{1,0:T(8,128)(2,1)S(1)}, bf16[512,1536]{1,0:T(8,128)(2,1)S(1)}, u32[]{:S(2)}, u32[]{:S(2)}) collective-permute-start(bf16[512,1536]{1,0:T(8,128)(2,1)S(1)} %get-tuple-element.33), channel_id=1, source_target_pairs={{0,1},{1,0},{2,3},{3,2},{4,5},{5,4},{6,7},{7,6},{8,9},{9,8},{10,11... | collective-permute-start | bytes 4718600 | tf_op jit(solution)/shard_map/ppermute | solution.py:45
  27.0 12.4 %collective-permute-start.6 = (bf16[128,2048]{1,0:T(8,128)(2,1)S(1)}, bf16[128,2048]{1,0:T(8,128)(2,1)S(1)}, u32[]{:S(2)}, u32[]{:S(2)}) collective-permute-start(bf16[128,2048]{1,0:T(8,128)(2,1)S(1)} %relay.22.refs_0_), channel_id=1, source_target_pairs={{0,2},{1,7},{2,4},{3,1},{4,6},{5,3},{6,0},{7,5},{8,10},{9,15},{10,... | collective-permute-start | bytes 1572872 | tf_op jit(solution)/shard_map/ppermute | solution.py:45
  30.8 12.3 %collective-permute-start.7 = (bf16[128,2048]{1,0:T(8,128)(2,1)S(1)}, bf16[128,2048]{1,0:T(8,128)(2,1)S(1)}, u32[]{:S(2)}, u32[]{:S(2)}) collective-permute-start(bf16[128,2048]{1,0:T(8,128)(2,1)S(1)} %relay.23.refs_0_), channel_id=1, source_target_pairs={{0,2},{1,7},{2,4},{3,1},{4,6},{5,3},{6,0},{7,5},{8,10},{9,15},{10,... | collective-permute-start | bytes 1572872 | tf_op jit(solution)/shard_map/ppermute | solution.py:45
  31.2 22.0 %collective-permute-start.10 = (bf16[512,1024]{1,0:T(8,128)(2,1)S(1)}, bf16[512,1024]{1,0:T(8,128)(2,1)S(1)}, u32[]{:S(2)}, u32[]{:S(2)}) collective-permute-start(bf16[512,1024]{1,0:T(8,128)(2,1)S(1)} %get-tuple-element.34), channel_id=1, source_target_pairs={{0,1},{1,0},{2,3},{3,2},{4,5},{5,4},{6,7},{7,6},{8,9},{9,8},{10,11... | collective-permute-start | bytes 3145736 | tf_op jit(solution)/shard_map/ppermute | solution.py:45
  34.7 13.6 %collective-permute-start.9 = (bf16[128,1536]{1,0:T(8,128)(2,1)S(1)}, bf16[128,1536]{1,0:T(8,128)(2,1)S(1)}, u32[]{:S(2)}, u32[]{:S(2)}) collective-permute-start(bf16[128,1536]{1,0:T(8,128)(2,1)S(1)} %relay.24.refs_0_), channel_id=1, source_target_pairs={{0,8},{1,25},{2,10},{3,27},{4,12},{5,29},{6,14},{7,31},{8,16},{9,1... | collective-permute-start | bytes 1179656 | tf_op jit(solution)/shard_map/ppermute | solution.py:45
  39.6 16.1 %collective-permute-start.11 = (bf16[128,2048]{1,0:T(8,128)(2,1)S(1)}, bf16[128,2048]{1,0:T(8,128)(2,1)S(1)}, u32[]{:S(2)}, u32[]{:S(2)}) collective-permute-start(bf16[128,2048]{1,0:T(8,128)(2,1)S(1)} %relay.25.refs_0_), channel_id=1, source_target_pairs={{0,2},{1,7},{2,4},{3,1},{4,6},{5,3},{6,0},{7,5},{8,10},{9,15},{10,... | collective-permute-start | bytes 1572872 | tf_op jit(solution)/shard_map/ppermute | solution.py:45
  43.3 12.4 %collective-permute-start.12 = (bf16[128,2048]{1,0:T(8,128)(2,1)S(1)}, bf16[128,2048]{1,0:T(8,128)(2,1)S(1)}, u32[]{:S(2)}, u32[]{:S(2)}) collective-permute-start(bf16[128,2048]{1,0:T(8,128)(2,1)S(1)} %relay.26.refs_0_), channel_id=1, source_target_pairs={{0,2},{1,7},{2,4},{3,1},{4,6},{5,3},{6,0},{7,5},{8,10},{9,15},{10,... | collective-permute-start | bytes 1572872 | tf_op jit(solution)/shard_map/ppermute | solution.py:45
  43.8 16.1 %collective-permute-start.13 = (bf16[128,1536]{1,0:T(8,128)(2,1)S(1)}, bf16[128,1536]{1,0:T(8,128)(2,1)S(1)}, u32[]{:S(2)}, u32[]{:S(2)}) collective-permute-start(bf16[128,1536]{1,0:T(8,128)(2,1)S(1)} %relay.27.refs_0_), channel_id=1, source_target_pairs={{0,2},{1,7},{2,4},{3,1},{4,6},{5,3},{6,0},{7,5},{8,10},{9,15},{10,... | collective-permute-start | bytes 1179656 | tf_op jit(solution)/shard_map/ppermute | solution.py:45
  48.5 14.9 %collective-permute-start.15 = (bf16[128,1536]{1,0:T(8,128)(2,1)S(1)}, bf16[128,1536]{1,0:T(8,128)(2,1)S(1)}, u32[]{:S(2)}, u32[]{:S(2)}) collective-permute-start(bf16[128,1536]{1,0:T(8,128)(2,1)S(1)} %relay.28.refs_0_), channel_id=1, source_target_pairs={{0,8},{1,25},{2,10},{3,27},{4,12},{5,29},{6,14},{7,31},{8,16},{9,1... | collective-permute-start | bytes 1179656 | tf_op jit(solution)/shard_map/ppermute | solution.py:45
  56.1 11.1 %collective-permute-start.16 = (bf16[32,4096]{1,0:T(8,128)(2,1)S(1)}, bf16[32,4096]{1,0:T(8,128)(2,1)S(1)}, u32[]{:S(2)}, u32[]{:S(2)}) collective-permute-start(bf16[32,4096]{1,0:T(8,128)(2,1)S(1)} %get-tuple-element.35.refs_0_), channel_id=1, source_target_pairs={{0,8},{1,25},{2,10},{3,27},{4,12},{5,29},{6,14},{7,31},{8,16},{9,1... | collective-permute-start | bytes 786440 | tf_op jit(solution)/shard_map/ppermute | solution.py:45
  60.1 11.9 %collective-permute-start.17 = (bf16[128,1536]{1,0:T(8,128)(2,1)S(1)}, bf16[128,1536]{1,0:T(8,128)(2,1)S(1)}, u32[]{:S(2)}, u32[]{:S(2)}) collective-permute-start(bf16[128,1536]{1,0:T(8,128)(2,1)S(1)} %relay.30.refs_0_), channel_id=1, source_target_pairs={{0,2},{1,7},{2,4},{3,1},{4,6},{5,3},{6,0},{7,5},{8,10},{9,15},{10,... | collective-permute-start | bytes 1179656 | tf_op jit(solution)/shard_map/ppermute | solution.py:45
  62.8 10.0 %collective-permute-start.18 = (bf16[128,1024]{1,0:T(8,128)(2,1)S(1)}, bf16[128,1024]{1,0:T(8,128)(2,1)S(1)}, u32[]{:S(2)}, u32[]{:S(2)}) collective-permute-start(bf16[128,1024]{1,0:T(8,128)(2,1)S(1)} %relay.31.refs_0_), channel_id=1, source_target_pairs={{0,2},{1,7},{2,4},{3,1},{4,6},{5,3},{6,0},{7,5},{8,10},{9,15},{10,... | collective-permute-start | bytes 786440 | tf_op jit(solution)/shard_map/ppermute | solution.py:45
  63.5 11.0 %collective-permute-start.19 = (bf16[32,1536]{1,0:T(8,128)(2,1)S(1)}, bf16[32,1536]{1,0:T(8,128)(2,1)S(1)}, u32[]{:S(2)}, u32[]{:S(2)}) collective-permute-start(bf16[32,1536]{1,0:T(8,128)(2,1)S(1)} %get-tuple-element.36.refs_0_), channel_id=1, source_target_pairs={{0,2},{1,7},{2,4},{3,1},{4,6},{5,3},{6,0},{7,5},{8,10},{9,15},{10,... | collective-permute-start | bytes 294920 | tf_op jit(solution)/shard_map/ppermute | solution.py:45
  67.3 10.2 %collective-permute-start.20 = (bf16[32,4096]{1,0:T(8,128)(2,1)S(1)}, bf16[32,4096]{1,0:T(8,128)(2,1)S(1)}, u32[]{:S(2)}, u32[]{:S(2)}) collective-permute-start(bf16[32,4096]{1,0:T(8,128)(2,1)S(1)} %relay.32.refs_0_), channel_id=1, source_target_pairs={{0,8},{1,25},{2,10},{3,27},{4,12},{5,29},{6,14},{7,31},{8,16},{9,1... | collective-permute-start | bytes 786440 | tf_op jit(solution)/shard_map/ppermute | solution.py:45
  72.1 13.1 %collective-permute-start.22 = (bf16[128,1536]{1,0:T(8,128)(2,1)S(1)}, bf16[128,1536]{1,0:T(8,128)(2,1)S(1)}, u32[]{:S(2)}, u32[]{:S(2)}) collective-permute-start(bf16[128,1536]{1,0:T(8,128)(2,1)S(1)} %relay.33.refs_0_), channel_id=1, source_target_pairs={{0,2},{1,7},{2,4},{3,1},{4,6},{5,3},{6,0},{7,5},{8,10},{9,15},{10,... | collective-permute-start | bytes 1179656 | tf_op jit(solution)/shard_map/ppermute | solution.py:45
  72.9 12.2 %collective-permute-start.23 = (bf16[128,1024]{1,0:T(8,128)(2,1)S(1)}, bf16[128,1024]{1,0:T(8,128)(2,1)S(1)}, u32[]{:S(2)}, u32[]{:S(2)}) collective-permute-start(bf16[128,1024]{1,0:T(8,128)(2,1)S(1)} %relay.34.refs_0_), channel_id=1, source_target_pairs={{0,2},{1,7},{2,4},{3,1},{4,6},{5,3},{6,0},{7,5},{8,10},{9,15},{10,... | collective-permute-start | bytes 786440 | tf_op jit(solution)/shard_map/ppermute | solution.py:45
  74.6 10.4 %collective-permute-start.21 = (bf16[32,1536]{1,0:T(8,128)(2,1)S(1)}, bf16[32,1536]{1,0:T(8,128)(2,1)S(1)}, u32[]{:S(2)}, u32[]{:S(2)}) collective-permute-start(bf16[32,1536]{1,0:T(8,128)(2,1)S(1)} %relay.35.refs_0_), channel_id=1, source_target_pairs={{0,2},{1,7},{2,4},{3,1},{4,6},{5,3},{6,0},{7,5},{8,10},{9,15},{10,... | collective-permute-start | bytes 294920 | tf_op jit(solution)/shard_map/ppermute | solution.py:45
  77.5 16.3 %collective-permute-start.24 = (bf16[32,4096]{1,0:T(8,128)(2,1)S(1)}, bf16[32,4096]{1,0:T(8,128)(2,1)S(1)}, u32[]{:S(2)}, u32[]{:S(2)}) collective-permute-start(bf16[32,4096]{1,0:T(8,128)(2,1)S(1)} %relay.36.refs_0_), channel_id=1, source_target_pairs={{0,8},{1,25},{2,10},{3,27},{4,12},{5,29},{6,14},{7,31},{8,16},{9,1... | collective-permute-start | bytes 786440 | tf_op jit(solution)/shard_map/ppermute | solution.py:45
  85.4 15.9 %collective-permute-start.26 = (bf16[32,2560]{1,0:T(8,128)(2,1)S(1)}, bf16[32,2560]{1,0:T(8,128)(2,1)S(1)}, u32[]{:S(2)}, u32[]{:S(2)}) collective-permute-start(bf16[32,2560]{1,0:T(8,128)(2,1)S(1)} %get-tuple-element.39.refs_0_), channel_id=1, source_target_pairs={{0,24},{1,9},{2,26},{3,11},{4,28},{5,13},{6,30},{7,15},{8,0},{9,17... | collective-permute-start | bytes 491528 | tf_op jit(solution)/shard_map/ppermute | solution.py:45
  85.5 15.8 %collective-permute-start.27 = (bf16[32,2560]{1,0:T(8,128)(2,1)S(1)}, bf16[32,2560]{1,0:T(8,128)(2,1)S(1)}, u32[]{:S(2)}, u32[]{:S(2)}) collective-permute-start(bf16[32,2560]{1,0:T(8,128)(2,1)S(1)} %get-tuple-element.41), channel_id=1, source_target_pairs={{0,16},{1,17},{2,18},{3,19},{4,20},{5,21},{6,22},{7,23},{8,24},{9,... | collective-permute-start | bytes 491528 | tf_op jit(solution)/shard_map/ppermute | solution.py:45
  87.9 13.9 %collective-permute-start.28 = (bf16[32,2560]{1,0:T(8,128)(2,1)S(1)}, bf16[32,2560]{1,0:T(8,128)(2,1)S(1)}, u32[]{:S(2)}, u32[]{:S(2)}) collective-permute-start(bf16[32,2560]{1,0:T(8,128)(2,1)S(1)} %get-tuple-element.42), channel_id=1, source_target_pairs={{0,8},{1,25},{2,10},{3,27},{4,12},{5,29},{6,14},{7,31},{8,16},{9,1... | collective-permute-start | bytes 491528 | tf_op jit(solution)/shard_map/ppermute | solution.py:45
  (14 other events, 110.3 us)
